TPU v7x, 256 devices: a whole 4x4x8 slice. The times are simulated.
256 devices in a mesh: member: 8 (over y, core), grid: 32 (over x, z).
Axes of the slice: x: 4, y: 4, z: 8, core: 2. Of those that a mesh axis runs over, the one named last changes fastest.
Arguments:
- prediction: float32 [8, 100, 131072], P('member', None, 'grid'), may hold values from -6 to 6
- reference_state: float32 [100, 131072], P(None, 'grid'), may hold values from -6 to 6
- quantity_penalty_factor: float32 [100], replicated, may hold values from 0.1 to 1
- point_surface_factor: float32 [131072], P('grid'), may hold values from 0.1 to 3
- latitude_row_start: int32 [33], replicated, may hold values from 0 to 65536, as said below
Outputs:
- scaled_derivative: float32 [8, 100, 65536], P('member', None, 'grid')
- loss: float32 [], replicated
Inputs may be any that keep to these rules, and one draw needn't show every extreme that they name: latitude_row_start[0] = 0, latitude_row_start[32] = 65536, and latitude_row_start[g] differs from g * 2048 by at most 1023; every band holds 2 to 4094 cells, and some band holds exactly 4094.
All inputs are finite; a program needn't handle non-finite values.
Results may differ from a plain program's by a relative error of at most 0.0003.
Values sent between devices are 32-bit elements; how exact they have to be, the bound alone decides.
A program may use at most 64 MiB of HBM per device.

v0:
```python
import jax
import jax.numpy as jnp
from jax import lax
from jax.sharding import PartitionSpec as P


def extended(cells, sides, width):
    for axis, dim in sides:
        count = lax.axis_size(axis)
        ends = count - 1
        head = lax.slice_in_dim(cells, 0, width, axis=dim)
        tail = lax.slice_in_dim(cells, cells.shape[dim] - width, cells.shape[dim], axis=dim)
        cells = jnp.concatenate(
            [
                lax.ppermute(tail, axis, [(i, (i + 1) % count) for i in range(ends)]),
                cells,
                lax.ppermute(head, axis, [((i + 1) % count, i) for i in range(ends)]),
            ],
            axis=dim,
        )
    return cells


def select_points(buffer, offsets, sender, uniform_points):
    last = buffer.ndim - 1
    first_run = lax.dynamic_slice_in_dim(buffer, offsets[0], uniform_points, last)
    own_run = lax.dynamic_slice_in_dim(buffer, offsets[1], uniform_points, last)
    next_run = lax.dynamic_slice_in_dim(buffer, offsets[2], uniform_points, last)
    return jnp.where(sender == 0, first_run, jnp.where(sender == 1, own_run, next_run))


def local(
    prediction, reference_state, quantity_penalty_factor, point_surface_factor, latitude_row_start
):
    members = lax.axis_size("member")
    groups = lax.axis_size("grid")
    quantity_accumulated = prediction.shape[1]
    points_in_latitude_row = prediction.shape[2]
    uniform_points = points_in_latitude_row // 2
    all_cells = uniform_points * groups
    grid_pos = lax.axis_index("grid")
    start_own = latitude_row_start[grid_pos]
    start_next = latitude_row_start[grid_pos + 1]
    start_prev = latitude_row_start[jnp.maximum(grid_pos - 1, 0)]
    first_cell = grid_pos * uniform_points
    cell_ids = first_cell + jnp.arange(uniform_points, dtype=jnp.int32)
    sender = (cell_ids >= start_own).astype(jnp.int32) + (cell_ids >= start_next).astype(jnp.int32)
    latitude_row_starts = (
        first_cell - start_prev,
        points_in_latitude_row + first_cell - start_own,
        2 * points_in_latitude_row + first_cell - start_next,
    )
    nearby_prediction, around_truth, around_area = (
        extended(prediction, (("grid", 2),), points_in_latitude_row),
        extended(reference_state[None], (("grid", 2),), points_in_latitude_row),
        extended(point_surface_factor[None, None], (("grid", 2),), points_in_latitude_row),
    )
    prediction_arrays = select_points(
        nearby_prediction, latitude_row_starts, sender, uniform_points
    )
    receiver = select_points(around_truth, latitude_row_starts, sender, uniform_points)[0]
    cell_weight = select_points(around_area, latitude_row_starts, sender, uniform_points)[0, 0]
    factors = quantity_penalty_factor[:, None] * cell_weight[None, :]
    scale = 1.0 / (quantity_accumulated * all_cells)
    whole_ensemble = lax.all_gather(prediction_arrays, "member", axis=0, tiled=True)
    self_quantity = prediction_arrays[0]
    member_pos = lax.axis_index("member")
    deviation = self_quantity[None] - whole_ensemble
    row_part = jnp.sum(factors[None] * deviation * deviation, axis=(1, 2))
    obs_part = jnp.sum(factors * (self_quantity - receiver) ** 2)
    row_sum, analysis_accumulated = lax.psum((row_part, obs_part), "grid")
    analysis_distance = jnp.sqrt(analysis_accumulated * scale + 1e-06)
    pair_dist = jnp.sqrt(row_sum * scale + 1e-06)
    offdiag = (jnp.arange(members, dtype=jnp.int32) != member_pos).astype(jnp.float32)
    reciprocal = offdiag / pair_dist
    blended = jnp.einsum("k,kvc->vc", reciprocal, whole_ensemble, precision=lax.Precision.HIGHEST)
    dispersion = self_quantity * jnp.sum(reciprocal) - blended
    result = (
        factors * ((self_quantity - receiver) / analysis_distance - dispersion / (members - 1))
    )[None]
    loss_part = analysis_distance / members - jnp.sum(offdiag * pair_dist) / (
        2.0 * members * (members - 1)
    )
    loss = lax.psum(loss_part, "member")
    return (result, loss)


def solution(mesh):
    placed = (P("member", None, "grid"), P(None, "grid"), P(), P("grid"), P())
    return jax.shard_map(
        local,
        mesh=mesh,
        in_specs=placed,
        out_specs=(P("member", None, "grid"), P()),
        check_vma=False,
    )
```

profile of v0, /device:TPU:1, one launch (start us, length us, event | category | flops | bytes accessed | tf_op | source)
XLA Modules:
  0.0 229.4 jit_solution(14967117893155267165)
XLA Ops:
  7.2 0.0 all-gather.2.cloned.1.call-start
  7.2 4.5 %collective-permute-start.2 = (f32[1,100,4096]{2,0,1:T(1,128)}, f32[1,100,4096]{2,0,1:T(1,128)S(1)}, u32[]{:S(2)}, u32[]{:S(2)}) collective-permute-start(f32[1,100,4096]{2,0,1:T(1,128)} %param.5), channel_id=1, source_target_pairs={{0,1},{1,2},{2,3},{3,4},{4,5},{5,6},{6,7},{7,8},{8,9},{9,10},{10,1... | collective-permute-start | bytes 4915208 | tf_op jit(solution)/shard_map/ppermute | solution.py:15
  11.7 1.3 collective-permute-start.3
  13.0 1.4 fusion.17
  16.4 1.3 fusion.8
  17.8 28.6 %collective-permute-done.2 = f32[1,100,4096]{2,0,1:T(1,128)S(1)} collective-permute-done((f32[1,100,4096]{2,0,1:T(1,128)}, f32[1,100,4096]{2,0,1:T(1,128)S(1)}, u32[]{:S(2)}, u32[]{:S(2)}) %collective-permute-start.2) | collective-permute-done | bytes 1638432 | tf_op jit(solution)/shard_map/ppermute | solution.py:15
  46.4 0.1 constant_dynamic-update-slice_fusion.2
  46.5 1.7 constant_dynamic-update-slice_fusion.1
  48.2 0.0 copy-start.1
  48.2 2.3 collective-permute-done.3
  50.4 1.7 constant_dynamic-update-slice_fusion
  52.1 0.0 copy-start.2
  52.1 5.1 %broadcast_select_fusion.1 = f32[1,100,2048]{2,0,1:T(1,128)S(1)} fusion(pred[2048]{0:T(1024)(128)(4,1)S(1)} %get-tuple-element.17, pred[2048]{0:T(1024)(128)(4,1)S(1)} %get-tuple-element.16, f32[1,100,12288]{2,0,1:T(1,128)S(1)} %constant_dynamic-update-slice_fusion, s32[]{:T(128)S(6)} %select_n.46, s32[]{:T(128)S(6)} %select_n.45, s32[]{:T(128)S(6)} %select_n.44), kind=kLoop, calls=%fused_computation.6 | loop fusion | flops 409600 | bytes 3280908 | tf_op jit(solution)/shard_map/jit(_where)/select_n | solution.py:29
  57.2 1.2 copy.29
  58.4 0.0 all-gather.2.cloned.1.call-update
  58.5 0.0 copy-done.1
  58.5 2.9 %copy.12 = f32[1,100,4096]{2,0,1:T(1,128)} copy(f32[1,100,4096]{2,1,0:T(8,128)S(1)} %bitcast.31) | data formatting | bytes 3276800 | tf_op jit(solution)/shard_map/broadcast_in_dim | solution.py:55
  61.3 4.8 %collective-permute-start.4 = (f32[1,100,4096]{2,0,1:T(1,128)}, f32[1,100,4096]{2,0,1:T(1,128)}, u32[]{:S(2)}, u32[]{:S(2)}) collective-permute-start(f32[1,100,4096]{2,0,1:T(1,128)} %copy.12), channel_id=1, source_target_pairs={{0,1},{1,2},{2,3},{3,4},{4,5},{5,6},{6,7},{7,8},{8,9},{9,10},{10,1... | collective-permute-start | bytes 4915208 | tf_op jit(solution)/shard_map/ppermute | solution.py:15
  66.1 1.3 collective-permute-start.5
  67.4 0.0 copy-done.2
  67.4 4.3 %collective-permute-start = (f32[1,1,4096]{2,1,0:T(1,128)S(1)}, f32[1,1,4096]{2,1,0:T(1,128)S(1)}, u32[]{:S(2)}, u32[]{:S(2)}) collective-permute-start(f32[1,1,4096]{2,1,0:T(1,128)S(1)} %bitcast.35), channel_id=1, source_target_pairs={{0,1},{1,2},{2,3},{3,4},{4,5},{5,6},{6,7},{7,8},{8,9},{9,10},{10,1... | collective-permute-start | bytes 49160 | tf_op jit(solution)/shard_map/ppermute | solution.py:15
  71.8 1.5 collective-permute-start.1
  73.3 25.7 %collective-permute-done = f32[1,1,4096]{2,1,0:T(1,128)S(1)} collective-permute-done((f32[1,1,4096]{2,1,0:T(1,128)S(1)}, f32[1,1,4096]{2,1,0:T(1,128)S(1)}, u32[]{:S(2)}, u32[]{:S(2)}) %collective-permute-start) | collective-permute-done | bytes 16416 | tf_op jit(solution)/shard_map/ppermute | solution.py:15
  99.0 5.8 %collective-permute-done.1 = f32[1,1,4096]{2,1,0:T(1,128)S(1)} collective-permute-done((f32[1,1,4096]{2,1,0:T(1,128)S(1)}, f32[1,1,4096]{2,1,0:T(1,128)S(1)}, u32[]{:S(2)}, u32[]{:S(2)}) %collective-permute-start.1) | collective-permute-done | bytes 16416 | tf_op jit(solution)/shard_map/ppermute | solution.py:17
  104.8 1.4 compare_select_fusion.1
  106.2 0.0 collective-permute-done.4
  106.3 2.6 %copy.14 = f32[1,100,4096]{2,1,0:T(8,128)S(1)} copy(f32[1,100,4096]{2,0,1:T(1,128)} %collective-permute-done.4) | data formatting | bytes 3276800 | tf_op jit(solution)/shard_map/ppermute | solution.py:15
  108.9 0.0 collective-permute-done.5
  108.9 2.6 %copy.15 = f32[1,100,4096]{2,1,0:T(8,128)S(1)} copy(f32[1,100,4096]{2,0,1:T(1,128)} %collective-permute-done.5) | data formatting | bytes 3276800 | tf_op jit(solution)/shard_map/ppermute | solution.py:17
  111.5 0.0 copy-start.3
  111.5 0.4 pad_maximum_fusion
  111.9 0.0 copy-start
  111.9 0.2 copy-done.3
  112.2 1.4 multiply_reduce_fusion
  113.5 0.0 all-gather.2.cloned.1.call-done
  113.5 0.0 copy-done
  113.5 4.0 %fusion = f32[8]{0:T(128)S(1)} fusion(f32[8,100,2048]{2,1,0:T(8,128)} %all-gather.2.cloned.1.call-done, f32[100,2048]{1,0:T(8,128)S(1)} %bitcast.30, f32[100,2048]{1,0:T(8,128)S(1)} %get-tuple-element.12), kind=kLoop, calls=%fused_computation.1 | loop fusion | flops 6553592 | bytes 8192032 | tf_op jit(solution)/shard_map/reduce_sum | solution.py:69
  117.6 58.7 %all-reduce = (f32[8]{0:T(128)S(1)}, f32[]{:T(128)}) all-reduce(f32[8]{0:T(128)S(1)} %fusion, f32[]{:T(128)} %get-tuple-element.8), channel_id=1, replica_groups=mesh['member'=8,'grid'=32] {'grid'}, use_global_device_ids=true, to_apply=%region_3.4 | all-reduce | flops 9 | bytes 72 | tf_op jit(solution)/shard_map/psum | solution.py:71
  176.9 0.6 fusion.13
  178.2 29.3 %psum.23 = f32[]{:T(128)} all-reduce(f32[]{:T(128)S(6)} %sub.42), channel_id=1, replica_groups=mesh['member'=8,'grid'=32] {'member'}, use_global_device_ids=true, to_apply=%region_6.7 | all-reduce | flops 1 | bytes 8 | tf_op jit(solution)/shard_map/psum | solution.py:84
  207.5 11.8 %fusion.1 = f32[1,100,2048]{2,0,1:T(1,128)S(1)} fusion(f32[8,100,2048]{2,1,0:T(8,128)} %all-gather.2.cloned.1.call-done, s32[]{:T(128)S(6)} %axis_index.25, f32[8]{0:T(128)S(1)} %get-tuple-element.6), kind=kOutput, calls=%fused_computation.2 | convolution fusion | flops 19660840 | bytes 7372836 | tf_op jit(solution)/shard_map/k,kvc->vc/dot_general | solution.py:76
  219.4 1.5 fusion.6
  220.8 1.7 copy.17
  (1 shorter events, 0.0 us)
Async XLA Ops:
  7.2 106.4 %all-gather.2.cloned.1.call-start = ((), (), s32[]{:S(2)}) async-start(), calls=%async_computation | async-start | bytes 7667712 | tf_op jit(solution)/shard_map/all_gather | solution.py:65
  7.2 39.1 %collective-permute-start.2 = (f32[1,100,4096]{2,0,1:T(1,128)}, f32[1,100,4096]{2,0,1:T(1,128)S(1)}, u32[]{:S(2)}, u32[]{:S(2)}) collective-permute-start(f32[1,100,4096]{2,0,1:T(1,128)} %param.5), channel_id=1, source_target_pairs={{0,1},{1,2},{2,3},{3,4},{4,5},{5,6},{6,7},{7,8},{8,9},{9,10},{10,1... | collective-permute-start | bytes 4915208 | tf_op jit(solution)/shard_map/ppermute | solution.py:15
  11.7 38.7 %collective-permute-start.3 = (f32[1,100,4096]{2,0,1:T(1,128)}, f32[1,100,4096]{2,0,1:T(1,128)}, u32[]{:S(2)}, u32[]{:S(2)}) collective-permute-start(f32[1,100,4096]{2,0,1:T(1,128)} %param.5), channel_id=1, source_target_pairs={{1,0},{2,1},{3,2},{4,3},{5,4},{6,5},{7,6},{8,7},{9,8},{10,9},{11,1... | collective-permute-start | bytes 4915208 | tf_op jit(solution)/shard_map/ppermute | solution.py:17
  48.2 10.3 %copy-start.1 = (f32[100,4096]{1,0:T(8,128)S(1)}, f32[100,4096]{1,0:T(8,128)}, u32[]{:S(2)}) copy-start(f32[100,4096]{1,0:T(8,128)} %param.6) | copy-start | bytes 4915204
  52.1 15.3 %copy-start.2 = (f32[4096]{0:T(1024)S(1)}, f32[4096]{0:T(1024)}, u32[]{:S(2)}) copy-start(f32[4096]{0:T(1024)} %param.8) | copy-start | bytes 49156
  61.3 44.9 %collective-permute-start.4 = (f32[1,100,4096]{2,0,1:T(1,128)}, f32[1,100,4096]{2,0,1:T(1,128)}, u32[]{:S(2)}, u32[]{:S(2)}) collective-permute-start(f32[1,100,4096]{2,0,1:T(1,128)} %copy.12), channel_id=1, source_target_pairs={{0,1},{1,2},{2,3},{3,4},{4,5},{5,6},{6,7},{7,8},{8,9},{9,10},{10,1... | collective-permute-start | bytes 4915208 | tf_op jit(solution)/shard_map/ppermute | solution.py:15
  66.1 42.7 %collective-permute-start.5 = (f32[1,100,4096]{2,0,1:T(1,128)}, f32[1,100,4096]{2,0,1:T(1,128)}, u32[]{:S(2)}, u32[]{:S(2)}) collective-permute-start(f32[1,100,4096]{2,0,1:T(1,128)} %copy.12), channel_id=1, source_target_pairs={{1,0},{2,1},{3,2},{4,3},{5,4},{6,5},{7,6},{8,7},{9,8},{10,9},{11,1... | collective-permute-start | bytes 4915208 | tf_op jit(solution)/shard_map/ppermute | solution.py:17
  67.4 31.5 %collective-permute-start = (f32[1,1,4096]{2,1,0:T(1,128)S(1)}, f32[1,1,4096]{2,1,0:T(1,128)S(1)}, u32[]{:S(2)}, u32[]{:S(2)}) collective-permute-start(f32[1,1,4096]{2,1,0:T(1,128)S(1)} %bitcast.35), channel_id=1, source_target_pairs={{0,1},{1,2},{2,3},{3,4},{4,5},{5,6},{6,7},{7,8},{8,9},{9,10},{10,1... | collective-permute-start | bytes 49160 | tf_op jit(solution)/shard_map/ppermute | solution.py:15
  71.8 33.0 %collective-permute-start.1 = (f32[1,1,4096]{2,1,0:T(1,128)S(1)}, f32[1,1,4096]{2,1,0:T(1,128)S(1)}, u32[]{:S(2)}, u32[]{:S(2)}) collective-permute-start(f32[1,1,4096]{2,1,0:T(1,128)S(1)} %bitcast.36), channel_id=1, source_target_pairs={{1,0},{2,1},{3,2},{4,3},{5,4},{6,5},{7,6},{8,7},{9,8},{10,9},{11,1... | collective-permute-start | bytes 49160 | tf_op jit(solution)/shard_map/ppermute | solution.py:17
  111.5 0.7 copy-start.3
  111.9 1.6 copy-start
Sparse Core Ops, SparseCore 0:
  58.6 49.9 all-gather.1
where the time goes:
time: 230 us; the launch traced here: 229 us
  blocking collectives  88 us (38%)
  waiting for transfers between devices  62.4 us (27%)
  starting transfers between devices  17.7 us (8%)
  between operations  17.6 us (8%)
  local copies, waits for them, and re-layouts  16.1 us (7%)
  other arithmetic  15.8 us (7%)
  matrix products  11.8 us (5%)
    psum x1, blocking collectives, local(): row_sum, analysis_accumulated = lax.psum((row_part, obs_part), 'grid')  58.7 us
    ppermute x3, waiting for transfers between devices, extended(): lax.ppermute(tail, axis, [(i, (i + 1) % count) for i in range(ends)])  54.3 us
    psum x1, blocking collectives, local(): loss = lax.psum(loss_part, 'member')  29.3 us
    ppermute x3, starting transfers between devices, extended(): lax.ppermute(tail, axis, [(i, (i + 1) % count) for i in range(ends)])  13.6 us
    dot_general x1, matrix products, local(): jnp.einsum('k,kvc->vc', reciprocal, whole_ensemble, precision=lax.Precisi...  11.8 us
    ppermute x3, waiting for transfers between devices, extended(): lax.ppermute(head, axis, [((i + 1) % count, i) for i in range(ends)])  8.06 us
    select_n x2, other arithmetic, select_points(): jnp.where(sender == 0, first_run, jnp.where(sender == 1, own_run, next_run))  6.57 us
    unnamed x12, local copies, waits for them, and re-layouts  4.93 us
  transfers between devices with their start and end apart: 7, of which 4 were waited for; matrix products, arithmetic and copies ran while one was open for 7% of the time, Pallas kernels for 0%

commit v1 on v0

v1 whole, which is shorter than its diff:
```python
import functools

import jax
import jax.numpy as jnp
from jax import lax
from jax.experimental import pallas as pl
from jax.experimental.pallas import tpu as pltpu
from jax.sharding import PartitionSpec as P

MESH = pl.DeviceIdType.MESH
F32 = jnp.float32
LANES = 128
CHUNKS = ((0, 5), (5, 11), (11, 18), (18, 25))
NX, NZ = 4, 8
NY, NC = 4, 2
MEMBERS = 8
GRID = 32
GROUPS = MEMBERS // 2
PAIRS = [(a, b) for a in range(MEMBERS) for b in range(a + 1, MEMBERS)]
ENTRIES = MEMBERS + len(PAIRS)


def align_kernel(
    starts,
    pred,
    truth,
    area,
    edge_out,
    own,
    y_out,
    y_own,
    xin,
    yin,
    win,
    edges,
    parts,
    y_edge,
    y_part,
    load_sem,
    save_sem,
):
    groups, share, tiles = pred.shape[:3]
    rows = groups * share
    edge = 8 * LANES
    half = 2 * edge
    lead = xin.shape[2] - tiles
    chunks = len(CHUNKS)
    m = lax.axis_index("member")
    g = lax.axis_index("grid")
    side, group = m // GROUPS, m % GROUPS
    row0 = group * share
    full = rows // 8 * 8
    spread = y_part.shape[0] // 8 - 1
    y_at = pl.multiple_of(group * 8, 8)
    y_span = share * 8 + 8

    x_loads = [
        pltpu.make_async_copy(
            pred.at[:, pl.ds(lo, hi - lo)],
            xin.at[:, pl.ds(lo, hi - lo), pl.ds(lead, tiles)],
            load_sem.at[c],
        )
        for c, (lo, hi) in enumerate(CHUNKS)
    ]
    y_load = pltpu.make_async_copy(truth, yin, load_sem.at[chunks])
    w_load = pltpu.make_async_copy(area, win.at[pl.ds(lead, tiles)], load_sem.at[chunks + 1])
    for copy in x_loads + [y_load, w_load]:
        copy.start()

    lo_cell = starts[g] - g * half
    shift = lo_cell + edge
    whole = lax.div(shift, LANES)
    part = lax.rem(shift, LANES)
    lane = lax.broadcasted_iota(jnp.int32, (8, LANES), 1)
    from_before = lane >= LANES - part

    def turned(now, before):
        return pltpu.roll(jnp.where(from_before, before, now), part, 1)

    def aligned(k, n, eighth):
        at = lead + 8 * eighth - whole
        return turned(xin[k, n, pl.ds(at, 8), :], xin[k, n, pl.ds(at - 1, 8), :])

    def aligned_area(eighth):
        at = lead + 8 * eighth - whole
        return turned(win[pl.ds(at, 8), :], win[pl.ds(at - 1, 8), :])

    def aligned_truth(eighth, put):
        for n in range(0, spread, 8):
            r = pl.multiple_of(jnp.minimum(row0 - group + n, full - 8), 8)

            def tile(t):
                at = lax.rem(8 * eighth + t - whole + 2 * tiles, tiles) * LANES
                cols = pl.ds(pl.multiple_of(at, LANES), LANES)
                value = yin[pl.ds(r, 8), cols]
                if n + 8 < spread:
                    return value
                rest = jnp.zeros((8 + full - rows, LANES), F32)
                tail = jnp.concatenate([yin[pl.ds(full, rows - full), cols], rest], axis=0)
                return jnp.where(group == GROUPS - 1, tail, value)

            before = tile(-1)
            for t in range(8):
                now = tile(t)
                put(n, t, turned(now, before))
                before = now

    saves = []
    for c, (lo, hi) in enumerate(CHUNKS):
        x_loads[c].wait()

        def align(n, _):
            for k in range(GROUPS):
                edges[k, n] = aligned(k, n, 3)
                edges[GROUPS + k, n] = aligned(k, n, 0)
                parts[k, n] = aligned(k, n, 1)
                parts[GROUPS + k, n] = aligned(k, n, 2)
            return 0

        lax.fori_loop(lo, hi, align, 0)
        for i, (src, dst) in enumerate(((edges, edge_out), (parts, own))):
            run = (slice(None), pl.ds(lo, hi - lo))
            saves.append(pltpu.make_async_copy(src.at[run], dst.at[run], save_sem.at[2 * c + i]))
            saves[-1].start()

    y_load.wait()
    w_load.wait()
    for i, (src, dst, eighth) in enumerate(((y_edge, y_out, 3 - 3 * side), (y_part, y_own, 1 + side))):

        def put(n, t, value):
            src[pl.ds(n * 8 + t, 8, stride=8), :] = value

        aligned_truth(eighth, put)
        src[pl.ds(y_at + share * 8, 8), :] = aligned_area(eighth)
        saves.append(
            pltpu.make_async_copy(src.at[pl.ds(y_at, y_span)], dst, save_sem.at[2 * chunks + i])
        )
        saves[-1].start()
    for copy in saves:
        copy.wait()


def exchange_kernel(
    starts,
    penalty,
    edge_out,
    own,
    y_out,
    truth,
    out,
    loss,
    edge_in,
    parts,
    xs,
    y_in,
    y_own,
    result,
    first,
    second,
    coef,
    load_sem,
    edge_send,
    edge_recv,
    y_send,
    y_recv,
    part_send,
    part_recv,
    own_sem,
    first_send,
    first_recv,
    second_send,
    second_recv,
    res_send,
    res_recv,
    keep_sem,
):
    share = parts.shape[1]
    rows = share * GROUPS
    edge = 8 * LANES
    half = 2 * edge
    m = lax.axis_index("member")
    g = lax.axis_index("grid")
    my, mc = m // NC, m % NC
    gx, gz = g // NZ, g % NZ
    side, group = m // GROUPS, m % GROUPS
    row0 = group * share

    def member_peer(p):
        return {"member": (m + p) % MEMBERS, "grid": g}

    def grid_peer(step):
        return {"member": m, "grid": (g + step + GRID) % GRID}

    def first_peer(p):
        return {"member": ((my + p // NX) % NY) * NC + mc, "grid": ((gx + p % NX) % NX) * NZ + gz}

    def second_peer(p):
        return {"member": my * NC + (mc + p % NC) % NC, "grid": gx * NZ + (gz + p // NC) % NZ}

    part_loads = [
        pltpu.make_async_copy(
            own.at[:, pl.ds(lo, hi - lo)], parts.at[:, pl.ds(lo, hi - lo)], load_sem.at[c]
        )
        for c, (lo, hi) in enumerate(CHUNKS)
    ]
    y_load = pltpu.make_async_copy(truth, y_own, load_sem.at[len(CHUNKS)])
    for copy in part_loads + [y_load]:
        copy.start()

    peers = [member_peer(p) for p in range(1, MEMBERS)]
    peers += [grid_peer(1), grid_peer(-1)]
    peers += [first_peer(p) for p in range(1, NX * NY)]
    peers += [second_peer(p) for p in range(1, NZ * NC)]
    barrier = pltpu.get_barrier_semaphore()
    for peer in peers:
        pl.semaphore_signal(barrier, inc=1, device_id=peer, device_id_type=MESH)

    lo_cell = starts[g] - g * half
    hi_cell = starts[g + 1] - g * half
    lane = lax.broadcasted_iota(jnp.int32, (8, LANES), 1)
    sub = lax.broadcasted_iota(jnp.int32, (8, LANES), 0)

    def edge_copy(c, s):
        lo, hi = CHUNKS[c]
        where = (pl.ds(s * GROUPS, GROUPS), pl.ds(lo, hi - lo))
        return pltpu.make_async_remote_copy(
            src_ref=edge_out.at[where],
            dst_ref=edge_in.at[where],
            send_sem=edge_send.at[c, s],
            recv_sem=edge_recv.at[c, s],
            device_id=grid_peer(1 if s == 0 else -1),
            device_id_type=MESH,
        )

    y_copy = pltpu.make_async_remote_copy(
        src_ref=y_out,
        dst_ref=y_in,
        send_sem=y_send,
        recv_sem=y_recv,
        device_id={"member": m, "grid": (g + 1 + side * (GRID - 2)) % GRID},
        device_id_type=MESH,
    )

    pl.semaphore_wait(barrier, len(peers))
    for c in range(len(CHUNKS)):
        for s in range(2):
            edge_copy(c, s).start()
        if c == 0:
            y_copy.start()

    def part_copy(c, p):
        lo, hi = CHUNKS[c]
        peer = member_peer(p)
        return pltpu.make_async_remote_copy(
            src_ref=parts.at[peer["member"], pl.ds(lo, hi - lo)],
            dst_ref=xs.at[m, pl.ds(lo, hi - lo)],
            send_sem=part_send.at[c, p],
            recv_sem=part_recv.at[c, p],
            device_id=peer,
            device_id_type=MESH,
        )

    def own_copy(c):
        lo, hi = CHUNKS[c]
        return pltpu.make_async_copy(
            parts.at[m, pl.ds(lo, hi - lo)], xs.at[m, pl.ds(lo, hi - lo)], own_sem.at[c]
        )

    def owned(s):
        cell = s * edge + sub * LANES + lane
        return (cell >= lo_cell) & (cell < hi_cell)

    in_half = [owned(0), owned(1)]
    for c, (lo, hi) in enumerate(CHUNKS):
        part_loads[c].wait()
        for s in range(2):
            edge_copy(c, s).wait_recv()

        def merge(n, _):
            for k in range(MEMBERS):
                parts[k, n] = jnp.where(in_half[k // GROUPS], parts[k, n], edge_in[k, n])
            return 0

        lax.fori_loop(lo, hi, merge, 0)
        for p in range(1, MEMBERS):
            part_copy(c, p).start()
        own_copy(c).start()

    y_load.wait()
    y_copy.wait_recv()
    in_own = owned(side)

    def merge_truth(n, _):
        at = pl.ds(pl.multiple_of(n * 8, 8), 8)
        y_own[at, :] = jnp.where(in_own, y_own[at, :], y_in[at, :])
        return 0

    lax.fori_loop(0, share + 1, merge_truth, 0)
    own_area = y_own[pl.ds(share * 8, 8), :]

    def load_row(n):
        x = [xs[k, n] for k in range(MEMBERS)]
        y = y_own[pl.ds(pl.multiple_of(n * 8, 8), 8), :]
        return x, y, penalty[row0 + n] * own_area

    sums = (jnp.zeros((8, LANES), F32),) * ENTRIES
    for c, (lo, hi) in enumerate(CHUNKS):
        own_copy(c).wait()
        for p in range(1, MEMBERS):
            part_copy(c, p).wait_recv()

        def add(n, sums):
            sums = list(sums)
            x, y, lw = load_row(n)
            for k in range(MEMBERS):
                d = x[k] - y
                sums[k] = sums[k] + lw * d * d
            for e, (a, b) in enumerate(PAIRS):
                d = x[a] - x[b]
                sums[MEMBERS + e] = sums[MEMBERS + e] + lw * d * d
            return tuple(sums)

        sums = lax.fori_loop(lo, hi, add, sums)

    message = jnp.zeros((8, LANES), F32)
    for e in range(0, ENTRIES, 8):
        column = [jnp.sum(s, axis=0, keepdims=True) for s in sums[e : e + 8]]
        column += [jnp.zeros((1, LANES), F32)] * (8 - len(column))
        total = jnp.sum(jnp.concatenate(column, axis=0), axis=1, keepdims=True)
        message = jnp.where(lane == e // 8, total, message)

    def exchange(message, buffer, send, recv, peer_of, count, place):
        buffer[place] = message
        copies = [
            pltpu.make_async_remote_copy(
                src_ref=buffer.at[place],
                dst_ref=buffer.at[place],
                send_sem=send.at[p],
                recv_sem=recv.at[p],
                device_id=peer_of(p),
                device_id_type=MESH,
            )
            for p in range(1, count)
        ]
        for copy in copies:
            copy.start()
        for copy in copies:
            copy.wait_recv()
        total = buffer[0]
        for i in range(1, count):
            total = total + buffer[i]
        return total, copies

    message, first_copies = exchange(
        message, first, first_send, first_recv, first_peer, NX * NY, my * NX + gx
    )
    message, second_copies = exchange(
        message, second, second_send, second_recv, second_peer, NZ * NC, gz * NC + mc
    )

    scale = 1.0 / (rows * half * GRID)
    distance = jnp.sqrt(message * scale + 1e-06)
    entry = lane * 8 + sub
    is_truth = entry < MEMBERS
    share_of = jnp.where(is_truth, 1.0 / MEMBERS, -1.0 / (MEMBERS * (MEMBERS - 1)))
    loss[...] = jnp.sum(jnp.where(entry < ENTRIES, distance * share_of, 0.0), keepdims=True)
    factor = jnp.where(is_truth, 1.0, 1.0 / (MEMBERS - 1)) / distance
    for e in range(ENTRIES):
        coef[e] = jnp.broadcast_to(factor[e % 8 : e % 8 + 1, e // 8 : e // 8 + 1], (8, LANES))

    def place_of(c):
        lo, hi = CHUNKS[c]
        return out.at[pl.ds(row0 + lo, hi - lo), pl.ds(pl.multiple_of(side * 8, 8), 8)]

    def res_copy(c, p):
        lo, hi = CHUNKS[c]
        peer = member_peer(p)
        return pltpu.make_async_remote_copy(
            src_ref=result.at[peer["member"], pl.ds(lo, hi - lo)],
            dst_ref=place_of(c),
            send_sem=res_send.at[c, p],
            recv_sem=res_recv.at[c, p],
            device_id=peer,
            device_id_type=MESH,
        )

    def keep_copy(c):
        lo, hi = CHUNKS[c]
        return pltpu.make_async_copy(
            result.at[m, pl.ds(lo, hi - lo)], place_of(c), keep_sem.at[c]
        )

    for c, (lo, hi) in enumerate(CHUNKS):

        def derive(n, _):
            x, y, lw = load_row(n)
            o = [(x[k] - y) * coef[k] for k in range(MEMBERS)]
            for e, (a, b) in enumerate(PAIRS):
                d = (x[a] - x[b]) * coef[MEMBERS + e]
                o[a] = o[a] - d
                o[b] = o[b] + d
            for k in range(MEMBERS):
                result[k, n] = lw * o[k]
            return 0

        lax.fori_loop(lo, hi, derive, 0)
        for p in range(1, MEMBERS):
            res_copy(c, p).start()
        keep_copy(c).start()

    for c in range(len(CHUNKS)):
        for s in range(2):
            edge_copy(c, s).wait_send()
        for p in range(1, MEMBERS):
            part_copy(c, p).wait_send()
    y_copy.wait_send()
    for copy in first_copies + second_copies:
        copy.wait_send()
    for c in range(len(CHUNKS)):
        keep_copy(c).wait()
        for p in range(1, MEMBERS):
            res_copy(c, p).wait_send()
            res_copy(c, p).wait_recv()


def local(prediction, reference_state, penalty, area, starts):
    rows, slots = prediction.shape[1:]
    tiles = slots // LANES
    share = rows // GROUPS
    spread = -(-(share + GROUPS - 1) // 8) * 8
    lead = tiles // 2 + 8
    chunks = len(CHUNKS)
    vmem = functools.partial(pltpu.VMEM, dtype=F32)
    array = functools.partial(jax.ShapeDtypeStruct, dtype=F32)
    dma = pltpu.SemaphoreType.DMA
    in_smem = pl.BlockSpec(memory_space=pltpu.SMEM)
    anywhere = pl.BlockSpec(memory_space=pl.ANY)
    fields = (MEMBERS, share, 8, LANES)
    y_share = (share * 8 + 8, LANES)
    y_spread = (spread * 8 + 8, LANES)
    aligned = pl.pallas_call(
        align_kernel,
        name="align",
        out_shape=(array(fields), array(fields), array(y_share), array(y_share)),
        in_specs=[in_smem, anywhere, anywhere, anywhere],
        out_specs=(anywhere,) * 4,
        scratch_shapes=[
            vmem((GROUPS, share, tiles + lead, LANES)),
            vmem((rows, slots)),
            vmem((tiles + lead, LANES)),
            vmem(fields),
            vmem(fields),
            vmem(y_spread),
            vmem(y_spread),
            dma((chunks + 2,)),
            dma((2 * chunks + 2,)),
        ],
        compiler_params=pltpu.CompilerParams(vmem_limit_bytes=40 * 2**20),
    )(
        starts,
        prediction.reshape(GROUPS, share, tiles, LANES),
        reference_state,
        area.reshape(tiles, LANES),
    )
    result, loss = pl.pallas_call(
        exchange_kernel,
        name="energy_score",
        out_shape=(array((rows, tiles // 2, LANES)), array((1, 1))),
        in_specs=[in_smem, in_smem] + [anywhere] * 4,
        out_specs=(anywhere, pl.BlockSpec(memory_space=pltpu.VMEM)),
        scratch_shapes=[
            vmem(fields),
            vmem(fields),
            vmem(fields),
            vmem(y_share),
            vmem(y_share),
            vmem(fields),
            vmem((NX * NY, 8, LANES)),
            vmem((NZ * NC, 8, LANES)),
            vmem((ENTRIES, 8, LANES)),
            dma((chunks + 1,)),
            dma((chunks, 2)),
            dma((chunks, 2)),
            dma,
            dma,
            dma((chunks, MEMBERS)),
            dma((chunks, MEMBERS)),
            dma((chunks,)),
            dma((NX * NY,)),
            dma((NX * NY,)),
            dma((NZ * NC,)),
            dma((NZ * NC,)),
            dma((chunks, MEMBERS)),
            dma((chunks, MEMBERS)),
            dma((chunks,)),
        ],
        compiler_params=pltpu.CompilerParams(
            collective_id=0, has_side_effects=True, vmem_limit_bytes=40 * 2**20
        ),
    )(starts, penalty, *aligned)
    return (result.reshape(1, rows, slots // 2), loss.reshape(()))


def solution(mesh):
    placed = (P("member", None, "grid"), P(None, "grid"), P(), P("grid"), P())
    return jax.shard_map(
        local,
        mesh=mesh,
        in_specs=placed,
        out_specs=(P("member", None, "grid"), P()),
        check_vma=False,
    )
```

time: 230 us -> 65.8 us (0.29)
  blocking collectives: 88 us -> 0 us
  waiting for transfers between devices: 62.4 us -> 0 us
  Pallas kernels: 0 us -> 57.9 us
  starting transfers between devices: 17.7 us -> 0 us
  other arithmetic: 15.8 us -> 0 us
  between operations: 17.6 us -> 2.49 us
  matrix products: 11.8 us -> 0 us
  local copies, waits for them, and re-layouts: 16.1 us -> 5.15 us
    psum x2 -> x0, blocking collectives: 88 us -> none  [the longest x1 58.7 us: local(): row_sum, analysis_accumulated = lax.psum((row_part, obs_part), 'grid')]
    ppermute x6 -> x0, waiting for transfers between devices: 62.3 us -> none  [the longest x3 54.3 us: extended(): lax.ppermute(tail, axis, [(i, (i + 1) % count) for i in range(ends)])]
    pallas_call x0 -> x2, Pallas kernels: none -> 57.9 us  [the longest x1 53.8 us: local(): pl.pallas_call(exchange_kernel, name='energy_score', out_shape=(array((ro...]
    ppermute x6 -> x0, starting transfers between devices: 17.7 us -> none  [the longest x3 13.6 us: extended(): lax.ppermute(tail, axis, [(i, (i + 1) % count) for i in range(ends)])]
    dot_general x1 -> x0, matrix products: 11.8 us -> none  [local(): jnp.einsum('k,kvc->vc', reciprocal, whole_ensemble, precision=lax.Precisi...]
    select_n x2 -> x0, other arithmetic: 6.57 us -> none  [select_points(): jnp.where(sender == 0, first_run, jnp.where(sender == 1, own_run, next_run))]
    reduce_sum x3 -> x0, other arithmetic: 6.02 us -> none  [the longest x1 4.03 us: local(): row_part = jnp.sum(factors[None] * deviation * deviation, axis=(1, 2))]
    ppermute x2 -> x0, local copies, waits for them, and re-layouts: 5.22 us -> none  [the longest x1 2.61 us: extended(): lax.ppermute(tail, axis, [(i, (i + 1) % count) for i in range(ends)])]
  transfers between devices with their start and end apart: 7 -> 0, of which waited for: 4 -> 0; matrix products, arithmetic and copies ran while one was open for 7% -> 0% of each run, Pallas kernels for 0% -> 0%
where the time goes in v1:
time: 65.8 us; the launch traced here: 65.6 us
  Pallas kernels  57.9 us (88%)
  local copies, waits for them, and re-layouts  5.15 us (8%)
  between operations  2.49 us (4%)
    pallas_call x1, Pallas kernels, local(): pl.pallas_call(exchange_kernel, name='energy_score', out_shape=(array((ro...  53.8 us
    unnamed x11, local copies, waits for them, and re-layouts  5.15 us
    pallas_call x1, Pallas kernels, local(): pl.pallas_call(align_kernel, name='align', out_shape=(array(fields), arra...  4.09 us

profile of v1, /device:TPU:1, one launch (start us, length us, event | category | flops | bytes accessed | tf_op | source)
XLA Modules:
  0.0 65.6 jit_solution(9905685574111842881)
XLA Ops:
  0.6 0.0 copy-start.4
  0.6 0.0 copy-start
  0.7 1.5 %copy-done = f32[100,4096]{1,0:T(8,128)S(1)} copy-done((f32[100,4096]{1,0:T(8,128)S(1)}, f32[100,4096]{1,0:T(8,128)}, u32[]{:S(2)}) %copy-start) | copy-done | bytes 1638424
  2.1 0.0 copy-start.1
  2.1 1.4 %copy-done.1 = f32[1,100,4096]{2,0,1:T(1,128)S(1)} copy-done((f32[1,100,4096]{2,0,1:T(1,128)S(1)}, f32[1,100,4096]{2,0,1:T(1,128)}, u32[]{:S(2)}) %copy-start.1) | copy-done | bytes 1638424
  3.5 0.0 copy-start.2
  3.5 0.7 %copy-done.2 = f32[4096]{0:T(1024)S(1)} copy-done((f32[4096]{0:T(1024)S(1)}, f32[4096]{0:T(1024)}, u32[]{:S(2)}) %copy-start.2) | copy-done | bytes 16408
  4.2 0.0 copy-start.3
  4.3 0.7 copy-done.3
  4.9 4.1 %align.1 = (f32[8,25,8,128]{3,2,1,0:T(8,128)S(1)}, f32[8,25,8,128]{3,2,1,0:T(8,128)S(1)}, f32[208,128]{1,0:T(8,128)S(1)}, f32[208,128]{1,0:T(8,128)S(1)}) custom-call(s32[33]{0:T(128)S(1)} %copy-done.3, f32[4,25,32,128]{3,2,1,0:T(8,128)S(1)} %bitcast.4, f32[100,4096]{1,0:T(8,128)S(1)} %copy-done, f32[32,128]{1,0:T(8,128)S(1)} %bitcast.6), custom_call_target="tpu_custom_call" | custom-call | tf_op jit(solution)/shard_map/align/pallas_call | solution.py:441
  9.0 0.0 copy-done.4
  9.0 53.8 %energy_score.1 = (f32[100,16,128]{2,1,0:T(8,128)S(1)}, f32[1,1]{1,0:T(1,128)}) custom-call(s32[33]{0:T(128)S(1)} %copy-done.3, f32[100]{0:T(128)S(1)} %copy-done.4, f32[8,25,8,128]{3,2,1,0:T(8,128)S(1)} %get-tuple-element.8.edge_out, f32[8,25,8,128]{3,2,1,0:T(8,128)S(1)} %get-tuple-element.9.own, f32[208,128]{1,0:T(8,128)S(1)} %get-tuple-element.10.y_out, ...), custom_call_target="tpu_custom_call" | custom-call | tf_op jit(solution)/shard_map/energy_score/pallas_call | solution.py:465
  62.8 0.9 %copy.11 = f32[1,100,2048]{2,0,1:T(1,128)} copy(f32[1,100,2048]{2,0,1:T(1,128)S(1)} %bitcast.5) | data formatting | bytes 1638400
Async XLA Ops:
  0.6 8.4 %copy-start.4 = (f32[100]{0:T(128)S(1)}, f32[100]{0:T(128)}, u32[]{:S(2)}) copy-start(f32[100]{0:T(128)} %penalty.1) | copy-start | bytes 1204
  0.6 1.5 %copy-start = (f32[100,4096]{1,0:T(8,128)S(1)}, f32[100,4096]{1,0:T(8,128)}, u32[]{:S(2)}) copy-start(f32[100,4096]{1,0:T(8,128)} %truth.1) | copy-start | bytes 4915204
  2.1 1.4 %copy-start.1 = (f32[1,100,4096]{2,0,1:T(1,128)S(1)}, f32[1,100,4096]{2,0,1:T(1,128)}, u32[]{:S(2)}) copy-start(f32[1,100,4096]{2,0,1:T(1,128)} %param.5) | copy-start | bytes 4915204
  3.5 0.7 %copy-start.2 = (f32[4096]{0:T(1024)S(1)}, f32[4096]{0:T(1024)}, u32[]{:S(2)}) copy-start(f32[4096]{0:T(1024)} %param.8) | copy-start | bytes 49156
  4.2 0.7 copy-start.3

commit v2 on v1

v2 whole, which is shorter than its diff:
```python
import functools

import jax
import jax.numpy as jnp
from jax import lax
from jax.experimental import pallas as pl
from jax.experimental.pallas import tpu as pltpu
from jax.sharding import PartitionSpec as P

MESH = pl.DeviceIdType.MESH
F32 = jnp.float32
LANES = 128
VMEM_BYTES = 62 * 2**20
CHUNKS = ((0, 5), (5, 10), (10, 15), (15, 20), (20, 25))
RETURNS = ((0, 3), (3, 12), (12, 25))
NX, NZ = 4, 8
NY, NC = 4, 2
MEMBERS = 8
GRID = 32
GROUPS = MEMBERS // 2
PAIRS = [(a, b) for a in range(MEMBERS) for b in range(a + 1, MEMBERS)]
ENTRIES = MEMBERS + len(PAIRS)


def kernel(
    starts,
    penalty,
    pred,
    truth,
    area,
    out,
    loss,
    xin,
    yin,
    win,
    y_rows,
    edge_out,
    edge_in,
    parts,
    xs,
    y_out,
    y_in,
    y_own,
    result,
    first,
    second,
    coef,
    load_sem,
    edge_send,
    edge_recv,
    y_send,
    y_recv,
    part_send,
    part_recv,
    own_sem,
    first_send,
    first_recv,
    second_send,
    second_recv,
    res_send,
    res_recv,
    keep_sem,
):
    share, tiles = pred.shape[1], pred.shape[2]
    rows = share * GROUPS
    edge = tiles // 4 * LANES
    half = 2 * edge
    chunks = len(CHUNKS)
    m = lax.axis_index("member")
    g = lax.axis_index("grid")
    my, mc = m // NC, m % NC
    gx, gz = g // NZ, g % NZ
    side, group = m // GROUPS, m % GROUPS
    row0 = group * share

    def member_peer(p):
        return {"member": (m + p) % MEMBERS, "grid": g}

    def grid_peer(step):
        return {"member": m, "grid": (g + step + GRID) % GRID}

    def first_peer(p):
        return {"member": ((my + p // NX) % NY) * NC + mc, "grid": ((gx + p % NX) % NX) * NZ + gz}

    def second_peer(p):
        return {"member": my * NC + (mc + p % NC) % NC, "grid": gx * NZ + (gz + p // NC) % NZ}

    x_loads = [
        pltpu.make_async_copy(
            pred.at[:, pl.ds(lo, hi - lo)], xin.at[:, pl.ds(lo, hi - lo)], load_sem.at[c]
        )
        for c, (lo, hi) in enumerate(CHUNKS)
    ]
    y_load = pltpu.make_async_copy(truth, yin, load_sem.at[chunks])
    w_load = pltpu.make_async_copy(area, win, load_sem.at[chunks + 1])
    for copy in x_loads + [y_load, w_load]:
        copy.start()

    peers = [member_peer(p) for p in range(1, MEMBERS)]
    peers += [grid_peer(1), grid_peer(-1)]
    peers += [first_peer(p) for p in range(1, NX * NY) if p % NX]
    peers += [second_peer(p) for p in range(NC, NZ * NC)]
    barrier = pltpu.get_barrier_semaphore()
    for peer in peers:
        pl.semaphore_signal(barrier, inc=1, device_id=peer, device_id_type=MESH)

    lo_cell = starts[g] - g * half
    hi_cell = starts[g + 1] - g * half
    shift = lo_cell + edge
    whole = lax.div(shift, LANES)
    part = lax.rem(shift, LANES)
    lane = lax.broadcasted_iota(jnp.int32, (8, LANES), 1)
    wrapped = lax.broadcasted_iota(jnp.int32, (tiles, LANES), 1) >= LANES - part

    def aligned(row):
        now = pltpu.roll(row, whole, 0)
        row = pltpu.roll(jnp.where(wrapped, pltpu.roll(now, 1, 0), now), part, 1)
        return [row[i : i + 8] for i in range(0, tiles, 8)]

    sub = lax.broadcasted_iota(jnp.int32, (8, LANES), 0)

    def edge_copy(c, s):
        lo, hi = CHUNKS[c]
        where = (pl.ds(s * GROUPS, GROUPS), pl.ds(lo, hi - lo))
        return pltpu.make_async_remote_copy(
            src_ref=edge_out.at[where],
            dst_ref=edge_in.at[where],
            send_sem=edge_send.at[c, s],
            recv_sem=edge_recv.at[c, s],
            device_id=grid_peer(1 if s == 0 else -1),
            device_id_type=MESH,
        )

    y_copy = pltpu.make_async_remote_copy(
        src_ref=y_out,
        dst_ref=y_in,
        send_sem=y_send,
        recv_sem=y_recv,
        device_id={"member": m, "grid": (g + 1 + side * (GRID - 2)) % GRID},
        device_id_type=MESH,
    )

    for c, (lo, hi) in enumerate(CHUNKS):
        x_loads[c].wait()

        def align(n, _):
            for k in range(GROUPS):
                before, left, right, after = aligned(xin[k, n])
                edge_out[k, n] = after
                edge_out[GROUPS + k, n] = before
                parts[k, n] = left
                parts[GROUPS + k, n] = right
            return 0

        lax.fori_loop(lo, hi, align, 0)
        if c == 0:
            pl.semaphore_wait(barrier, len(peers))
        for s in range(2):
            edge_copy(c, s).start()

    y_load.wait()
    w_load.wait()
    full = rows // 8 * 8
    spread = y_rows.shape[0] // tiles

    def turn(t, _):
        cols = pl.ds(pl.multiple_of(t * LANES, LANES), LANES)
        for n in range(0, spread, 8):
            r = pl.multiple_of(jnp.minimum(row0 - group + n, full - 8), 8)
            value = yin[pl.ds(r, 8), cols]
            if n + 8 == spread:
                rest = jnp.zeros((8 + full - rows, LANES), F32)
                tail = jnp.concatenate([yin[pl.ds(full, rows - full), cols], rest], axis=0)
                value = jnp.where(group == GROUPS - 1, tail, value)
            y_rows[pl.ds(n * tiles + t, 8, stride=tiles), :] = value
        return 0

    lax.fori_loop(0, tiles, turn, 0)

    def put_truth(n, row):
        before, left, right, after = aligned(row)
        y_out[n] = jnp.where(side == 0, after, before)
        y_own[n] = jnp.where(side == 0, left, right)

    def align_truth(n, _):
        put_truth(n, y_rows[pl.ds(pl.multiple_of((group + n) * tiles, tiles), tiles), :])
        return 0

    lax.fori_loop(0, share, align_truth, 0)
    put_truth(share, win[...])
    y_copy.start()

    def part_copy(c, p):
        lo, hi = CHUNKS[c]
        peer = member_peer(p)
        return pltpu.make_async_remote_copy(
            src_ref=parts.at[peer["member"], pl.ds(lo, hi - lo)],
            dst_ref=xs.at[m, pl.ds(lo, hi - lo)],
            send_sem=part_send.at[c, p],
            recv_sem=part_recv.at[c, p],
            device_id=peer,
            device_id_type=MESH,
        )

    def own_copy(c):
        lo, hi = CHUNKS[c]
        return pltpu.make_async_copy(
            parts.at[m, pl.ds(lo, hi - lo)], xs.at[m, pl.ds(lo, hi - lo)], own_sem.at[c]
        )

    def owned(s):
        cell = s * edge + sub * LANES + lane
        return (cell >= lo_cell) & (cell < hi_cell)

    in_half = [owned(0), owned(1)]
    for c, (lo, hi) in enumerate(CHUNKS):
        for s in range(2):
            edge_copy(c, s).wait_recv()

        def merge(n, _):
            for k in range(MEMBERS):
                parts[k, n] = jnp.where(in_half[k // GROUPS], parts[k, n], edge_in[k, n])
            return 0

        lax.fori_loop(lo, hi, merge, 0)
        for p in range(1, MEMBERS):
            part_copy(c, p).start()
        own_copy(c).start()

    y_copy.wait_recv()
    in_own = owned(side)

    def merge_truth(n, _):
        y_own[n] = jnp.where(in_own, y_own[n], y_in[n])
        return 0

    lax.fori_loop(0, share + 1, merge_truth, 0)
    own_area = y_own[share]

    def load_row(n):
        x = [xs[k, n] for k in range(MEMBERS)]
        y = y_own[n]
        return x, y, penalty[row0 + n] * own_area

    sums = (jnp.zeros((8, LANES), F32),) * ENTRIES
    for c, (lo, hi) in enumerate(CHUNKS):
        own_copy(c).wait()
        for p in range(1, MEMBERS):
            part_copy(c, p).wait_recv()

        def add(n, sums):
            sums = list(sums)
            x, y, lw = load_row(n)
            for k in range(MEMBERS):
                d = x[k] - y
                sums[k] = sums[k] + lw * d * d
            for e, (a, b) in enumerate(PAIRS):
                d = x[a] - x[b]
                sums[MEMBERS + e] = sums[MEMBERS + e] + lw * d * d
            return tuple(sums)

        sums = lax.fori_loop(lo, hi, add, sums)

    message = jnp.zeros((8, LANES), F32)
    for e in range(0, ENTRIES, 8):
        column = [jnp.sum(s, axis=0, keepdims=True) for s in sums[e : e + 8]]
        column += [jnp.zeros((1, LANES), F32)] * (8 - len(column))
        total = jnp.sum(jnp.concatenate(column, axis=0), axis=1, keepdims=True)
        message = jnp.where(lane == e // 8, total, message)

    def exchange(message, buffer, send, recv, peer_of, count, place):
        buffer[place] = message
        copies = [
            pltpu.make_async_remote_copy(
                src_ref=buffer.at[place],
                dst_ref=buffer.at[place],
                send_sem=send.at[p],
                recv_sem=recv.at[p],
                device_id=peer_of(p),
                device_id_type=MESH,
            )
            for p in range(1, count)
        ]
        for copy in copies:
            copy.start()
        for copy in copies:
            copy.wait_recv()
        total = buffer[0]
        for i in range(1, count):
            total = total + buffer[i]
        return total, copies

    message, first_copies = exchange(
        message, first, first_send, first_recv, first_peer, NX * NY, my * NX + gx
    )
    message, second_copies = exchange(
        message, second, second_send, second_recv, second_peer, NZ * NC, gz * NC + mc
    )

    scale = 1.0 / (rows * half * GRID)
    distance = jnp.sqrt(message * scale + 1e-06)
    entry = lane * 8 + sub
    is_truth = entry < MEMBERS
    share_of = jnp.where(is_truth, 1.0 / MEMBERS, -1.0 / (MEMBERS * (MEMBERS - 1)))
    loss[...] = jnp.sum(jnp.where(entry < ENTRIES, distance * share_of, 0.0), keepdims=True)
    factor = jnp.where(is_truth, 1.0, 1.0 / (MEMBERS - 1)) / distance
    for e in range(ENTRIES):
        coef[e] = jnp.broadcast_to(factor[e % 8 : e % 8 + 1, e // 8 : e // 8 + 1], (8, LANES))

    def place_of(c):
        lo, hi = RETURNS[c]
        return out.at[pl.ds(row0 + lo, hi - lo), pl.ds(pl.multiple_of(side * 8, 8), 8)]

    def res_copy(c, p):
        lo, hi = RETURNS[c]
        peer = member_peer(p)
        return pltpu.make_async_remote_copy(
            src_ref=result.at[peer["member"], pl.ds(lo, hi - lo)],
            dst_ref=place_of(c),
            send_sem=res_send.at[c, p],
            recv_sem=res_recv.at[c, p],
            device_id=peer,
            device_id_type=MESH,
        )

    def keep_copy(c):
        lo, hi = RETURNS[c]
        return pltpu.make_async_copy(
            result.at[m, pl.ds(lo, hi - lo)], place_of(c), keep_sem.at[c]
        )

    for c, (lo, hi) in enumerate(RETURNS):

        def derive(n, _):
            x, y, lw = load_row(n)
            o = [(x[k] - y) * coef[k] for k in range(MEMBERS)]
            for e, (a, b) in enumerate(PAIRS):
                d = (x[a] - x[b]) * coef[MEMBERS + e]
                o[a] = o[a] - d
                o[b] = o[b] + d
            for k in range(MEMBERS):
                result[k, n] = lw * o[k]
            return 0

        lax.fori_loop(lo, hi, derive, 0)
        for p in range(1, MEMBERS):
            res_copy(c, p).start()
        keep_copy(c).start()

    for c in range(chunks):
        for s in range(2):
            edge_copy(c, s).wait_send()
        for p in range(1, MEMBERS):
            part_copy(c, p).wait_send()
    y_copy.wait_send()
    for copy in first_copies + second_copies:
        copy.wait_send()
    for c in range(len(RETURNS)):
        keep_copy(c).wait()
        for p in range(1, MEMBERS):
            res_copy(c, p).wait_send()
            res_copy(c, p).wait_recv()


def local(prediction, reference_state, penalty, area, starts):
    rows, slots = prediction.shape[1:]
    tiles = slots // LANES
    share = rows // GROUPS
    spread = -(-(share + GROUPS - 1) // 8) * 8
    chunks, returns = len(CHUNKS), len(RETURNS)
    vmem = functools.partial(pltpu.VMEM, dtype=F32)
    array = functools.partial(jax.ShapeDtypeStruct, dtype=F32)
    dma = pltpu.SemaphoreType.DMA
    in_smem = pl.BlockSpec(memory_space=pltpu.SMEM)
    anywhere = pl.BlockSpec(memory_space=pl.ANY)
    fields = (MEMBERS, share, 8, LANES)
    y_share = (share + 1, 8, LANES)
    result, loss = pl.pallas_call(
        kernel,
        name="energy_score",
        out_shape=(array((rows, tiles // 2, LANES)), array((1, 1))),
        in_specs=[in_smem, in_smem, anywhere, anywhere, anywhere],
        out_specs=(anywhere, pl.BlockSpec(memory_space=pltpu.VMEM)),
        scratch_shapes=[
            vmem((GROUPS, share, tiles, LANES)),
            vmem((rows, slots)),
            vmem((tiles, LANES)),
            vmem((spread * tiles, LANES)),
            vmem(fields),
            vmem(fields),
            vmem(fields),
            vmem(fields),
            vmem(y_share),
            vmem(y_share),
            vmem(y_share),
            vmem(fields),
            vmem((NX * NY, 8, LANES)),
            vmem((NZ * NC, 8, LANES)),
            vmem((ENTRIES, 8, LANES)),
            dma((chunks + 2,)),
            dma((chunks, 2)),
            dma((chunks, 2)),
            dma,
            dma,
            dma((chunks, MEMBERS)),
            dma((chunks, MEMBERS)),
            dma((chunks,)),
            dma((NX * NY,)),
            dma((NX * NY,)),
            dma((NZ * NC,)),
            dma((NZ * NC,)),
            dma((returns, MEMBERS)),
            dma((returns, MEMBERS)),
            dma((returns,)),
        ],
        compiler_params=pltpu.CompilerParams(
            collective_id=0, has_side_effects=True, vmem_limit_bytes=VMEM_BYTES
        ),
    )(
        starts,
        penalty,
        prediction.reshape(GROUPS, share, tiles, LANES),
        reference_state,
        area.reshape(tiles, LANES),
    )
    return (result.reshape(1, rows, slots // 2), loss.reshape(()))


def solution(mesh):
    placed = (P("member", None, "grid"), P(None, "grid"), P(), P("grid"), P())
    return jax.shard_map(
        local,
        mesh=mesh,
        in_specs=placed,
        out_specs=(P("member", None, "grid"), P()),
        check_vma=False,
    )
```

time: 65.8 us -> 56.9 us (0.86)
  Pallas kernels: 57.9 us -> 52.3 us
  local copies, waits for them, and re-layouts: 5.15 us -> 2.09 us
    pallas_call x2 -> x1, Pallas kernels: 57.9 us -> 52.3 us  [local(): pl.pallas_call(kernel, name='energy_score', out_shape=(array((rows, tiles...]
    unnamed x11 -> x1, local copies, waits for them, and re-layouts: 5.15 us -> 2.09 us
where the time goes in v2:
time: 56.9 us; the launch traced here: 56.8 us
  Pallas kernels  52.3 us (92%)
  between operations  2.39 us (4%)
  local copies, waits for them, and re-layouts  2.09 us (4%)
    pallas_call x1, Pallas kernels, local(): pl.pallas_call(kernel, name='energy_score', out_shape=(array((rows, tiles...  52.3 us
    unnamed x1, local copies, waits for them, and re-layouts  2.09 us

profile of v2, /device:TPU:1, one launch (start us, length us, event | category | flops | bytes accessed | tf_op | source)
XLA Modules:
  0.0 56.8 jit_solution(7161953576727662692)
XLA Ops:
  0.6 52.3 %energy_score.1 = (f32[100,16,128]{2,1,0:T(8,128)}, f32[1,1]{1,0:T(1,128)}) custom-call(s32[33]{0:T(128)} %starts.1, f32[100]{0:T(128)} %penalty.1, f32[4,25,32,128]{3,2,1,0:T(8,128)} %bitcast.4, f32[100,4096]{1,0:T(8,128)} %truth.1, f32[32,128]{1,0:T(8,128)} %bitcast.6), custom_call_target="tpu_custom_call" | custom-call | tf_op jit(solution)/shard_map/energy_score/pallas_call | solution.py:378
  52.9 2.1 %copy.11 = f32[1,100,2048]{2,0,1:T(1,128)} copy(f32[1,100,2048]{2,0,1:T(1,128)} %bitcast.5) | data formatting | bytes 1638400

commit v3 on v2

--- a/solution.py
+++ b/solution.py
@@ -10,7 +10,7 @@
 MESH = pl.DeviceIdType.MESH
 F32 = jnp.float32
 LANES = 128
-VMEM_BYTES = 62 * 2**20
+VMEM_BYTES = 56 * 2**20
 CHUNKS = ((0, 5), (5, 10), (10, 15), (15, 20), (20, 25))
 RETURNS = ((0, 3), (3, 12), (12, 25))
 NX, NZ = 4, 8
@@ -20,6 +20,15 @@
 GROUPS = MEMBERS // 2
 PAIRS = [(a, b) for a in range(MEMBERS) for b in range(a + 1, MEMBERS)]
 ENTRIES = MEMBERS + len(PAIRS)
+
+
+def ring(step, count):
+    return min(step, count - step)
+
+
+FIRST = sorted(range(1, NX * NY), key=lambda p: -ring(p // NX, NY) - ring(p % NX, NX))
+SECOND = sorted(range(1, NZ * NC), key=lambda p: (-ring(p // NC, NZ), -(p % NC)))
+PEERS = sorted(range(1, MEMBERS), key=lambda p: -ring(p // NC, NY))
 
 
 def kernel(
@@ -223,7 +232,7 @@
             return 0
 
         lax.fori_loop(lo, hi, merge, 0)
-        for p in range(1, MEMBERS):
+        for p in PEERS:
             part_copy(c, p).start()
         own_copy(c).start()
 
@@ -268,7 +277,7 @@
         total = jnp.sum(jnp.concatenate(column, axis=0), axis=1, keepdims=True)
         message = jnp.where(lane == e // 8, total, message)
 
-    def exchange(message, buffer, send, recv, peer_of, count, place):
+    def exchange(message, buffer, send, recv, peer_of, order, place):
         buffer[place] = message
         copies = [
             pltpu.make_async_remote_copy(
@@ -279,22 +288,22 @@
                 device_id=peer_of(p),
                 device_id_type=MESH,
             )
-            for p in range(1, count)
+            for p in order
         ]
         for copy in copies:
             copy.start()
         for copy in copies:
             copy.wait_recv()
         total = buffer[0]
-        for i in range(1, count):
+        for i in range(1, len(order) + 1):
             total = total + buffer[i]
         return total, copies
 
     message, first_copies = exchange(
-        message, first, first_send, first_recv, first_peer, NX * NY, my * NX + gx
+        message, first, first_send, first_recv, first_peer, FIRST, my * NX + gx
     )
     message, second_copies = exchange(
-        message, second, second_send, second_recv, second_peer, NZ * NC, gz * NC + mc
+        message, second, second_send, second_recv, second_peer, SECOND, gz * NC + mc
     )
 
     scale = 1.0 / (rows * half * GRID)
@@ -343,7 +352,7 @@
             return 0
 
         lax.fori_loop(lo, hi, derive, 0)
-        for p in range(1, MEMBERS):
+        for p in PEERS:
             res_copy(c, p).start()
         keep_copy(c).start()
 
@@ -378,7 +387,7 @@
     result, loss = pl.pallas_call(
         kernel,
         name="energy_score",
-        out_shape=(array((rows, tiles // 2, LANES)), array((1, 1))),
+        out_shape=(pltpu.VMEM((rows, tiles // 2, LANES), F32), array((1, 1))),
         in_specs=[in_smem, in_smem, anywhere, anywhere, anywhere],
         out_specs=(anywhere, pl.BlockSpec(memory_space=pltpu.VMEM)),
         scratch_shapes=[

time: 56.9 us -> 54.2 us (0.953)
  Pallas kernels: 52.3 us -> 50.9 us
  local copies, waits for them, and re-layouts: 2.09 us -> 0.89 us
    pallas_call x1, Pallas kernels: 52.3 us -> 50.9 us  [local(): pl.pallas_call(kernel, name='energy_score', out_shape=(pltpu.VMEM((rows,...]
    unnamed x1, local copies, waits for them, and re-layouts: 2.09 us -> 0.89 us
where the time goes in v3:
time: 54.2 us; the launch traced here: 54.1 us
  Pallas kernels  50.9 us (94%)
  between operations  2.33 us (4%)
  local copies, waits for them, and re-layouts  0.89 us (2%)
    pallas_call x1, Pallas kernels, local(): pl.pallas_call(kernel, name='energy_score', out_shape=(pltpu.VMEM((rows,...  50.9 us

profile of v3, /device:TPU:1, one launch (start us, length us, event | category | flops | bytes accessed | tf_op | source)
XLA Modules:
  0.0 54.1 jit_solution(15327681384360157365)
XLA Ops:
  0.6 50.9 %energy_score.1 = (f32[100,16,128]{2,1,0:T(8,128)S(1)}, f32[1,1]{1,0:T(1,128)}) custom-call(s32[33]{0:T(128)} %starts.1, f32[100]{0:T(128)} %penalty.1, f32[4,25,32,128]{3,2,1,0:T(8,128)} %bitcast.5, f32[100,4096]{1,0:T(8,128)} %truth.1, f32[32,128]{1,0:T(8,128)} %bitcast.6), custom_call_target="tpu_custom_call" | custom-call | tf_op jit(solution)/shard_map/energy_score/pallas_call | solution.py:387
  51.5 0.9 %copy.11 = f32[1,100,2048]{2,0,1:T(1,128)} copy(f32[1,100,2048]{2,0,1:T(1,128)S(1)} %bitcast.4) | data formatting | bytes 1638400

commit v4 on v3

v4 whole, which is shorter than its diff:
```python
import functools

import jax
import jax.numpy as jnp
from jax import lax
from jax.experimental import pallas as pl
from jax.experimental.pallas import tpu as pltpu
from jax.sharding import PartitionSpec as P

MESH = pl.DeviceIdType.MESH
F32 = jnp.float32
LANES = 128
VMEM_BYTES = 56 * 2**20
CHUNKS = 5
RETURNS = 5
NX, NZ = 4, 8
NY, NC = 4, 2
MEMBERS = 8
GRID = 32
GROUPS = MEMBERS // 2
PAIRS = [(a, b) for a in range(MEMBERS) for b in range(a + 1, MEMBERS)]
ENTRIES = MEMBERS + len(PAIRS)


def ring(step, count):
    return min(step, count - step)


MEMBER_STEPS = ((0, 1), (2, 0), (1, 0), (3, 0), (2, 1), (1, 1), (3, 1))
FIRST_STEPS = sorted(
    [(y, x) for y in range(NY) for x in range(NX) if y or x],
    key=lambda s: -ring(s[0], NY) - ring(s[1], NX),
)
SECOND_STEPS = sorted(
    [(z, core) for z in range(NZ) for core in range(NC) if z or core],
    key=lambda s: (-ring(s[0], NZ), -s[1]),
)


def repeat(count, body):
    def step(i, carry):
        body(i)
        return carry

    lax.fori_loop(0, count, step, 0)


def kernel(
    starts_in,
    penalty_in,
    pred,
    truth,
    area,
    out,
    loss_out,
    starts,
    penalty,
    loss,
    xin,
    yin,
    win,
    y_rows,
    edge_out,
    edge_in,
    parts,
    xs,
    y_out,
    y_in,
    y_own,
    result,
    first,
    second,
    coef,
    load_sem,
    edge_send,
    edge_recv,
    y_send,
    y_recv,
    part_send,
    part_recv,
    own_sem,
    first_send,
    first_recv,
    second_send,
    second_recv,
    res_send,
    res_recv,
    keep_sem,
    loss_sem,
):
    share, tiles = pred.shape[1], pred.shape[2]
    rows = share * GROUPS
    edge = tiles // 4 * LANES
    half = 2 * edge
    run = share // CHUNKS
    m = lax.axis_index("member")
    g = lax.axis_index("grid")
    my, mc = m // NC, m % NC
    gx, gz = g // NZ, g % NZ
    side, group = m // GROUPS, m % GROUPS
    row0 = group * share

    def moved(z=0, y=0, x=0, core=0):
        member = ((my + y) % NY) * NC + (mc + core) % NC
        return {"member": member, "grid": ((gx + x) % NX) * NZ + (gz + z) % NZ}

    def member_peer(i):
        y, core = MEMBER_STEPS[i]
        y = (y + mc * (NY - 2 * y)) % NY
        return moved(y=y, core=core)

    def grid_peer(step):
        return {"member": m, "grid": (g + step + GRID) % GRID}

    def first_peer(i):
        y, x = FIRST_STEPS[i]
        return moved(y=y, x=x)

    def second_peer(i):
        z, core = SECOND_STEPS[i]
        return moved(z=z, core=core)

    meet = [(ring(z, NZ), moved(z=z, core=core)) for z, core in SECOND_STEPS if z]
    meet += [(ring(y, NY) + ring(x, NX), moved(y=y, x=x)) for y, x in FIRST_STEPS if x]
    meet += [(ring(y, NY), moved(y=y, core=core)) for y, core in MEMBER_STEPS]
    meet += [(2, grid_peer(1)), (2, grid_peer(-1))]
    barrier = pltpu.get_barrier_semaphore()
    for _, peer in sorted(meet, key=lambda entry: -entry[0]):
        pl.semaphore_signal(barrier, inc=1, device_id=peer, device_id_type=MESH)

    def rows_of(c):
        return pl.ds(c * run, run)

    def x_load(c):
        return pltpu.make_async_copy(
            pred.at[:, rows_of(c)], xin.at[:, rows_of(c)], load_sem.at[c]
        )

    y_load = pltpu.make_async_copy(truth, yin, load_sem.at[CHUNKS])
    w_load = pltpu.make_async_copy(area, win, load_sem.at[CHUNKS + 1])
    starts_load = pltpu.make_async_copy(starts_in, starts, load_sem.at[CHUNKS + 2])
    penalty_load = pltpu.make_async_copy(penalty_in, penalty, load_sem.at[CHUNKS + 3])
    starts_load.start()
    repeat(CHUNKS, lambda c: x_load(c).start())
    for copy in (y_load, w_load, penalty_load):
        copy.start()

    starts_load.wait()
    lo_cell = starts[g] - g * half
    hi_cell = starts[g + 1] - g * half
    shift = lo_cell + edge
    whole = lax.div(shift, LANES)
    part = lax.rem(shift, LANES)
    lane = lax.broadcasted_iota(jnp.int32, (8, LANES), 1)
    wrapped = lax.broadcasted_iota(jnp.int32, (tiles, LANES), 1) >= LANES - part

    def aligned(row):
        now = pltpu.roll(row, whole, 0)
        row = pltpu.roll(jnp.where(wrapped, pltpu.roll(now, 1, 0), now), part, 1)
        return [row[i : i + 8] for i in range(0, tiles, 8)]

    sub = lax.broadcasted_iota(jnp.int32, (8, LANES), 0)

    def edge_copy(c, s):
        where = (pl.ds(s * GROUPS, GROUPS), rows_of(c))
        return pltpu.make_async_remote_copy(
            src_ref=edge_out.at[where],
            dst_ref=edge_in.at[where],
            send_sem=edge_send.at[c, s],
            recv_sem=edge_recv.at[c, s],
            device_id=grid_peer(1 if s == 0 else -1),
            device_id_type=MESH,
        )

    y_copy = pltpu.make_async_remote_copy(
        src_ref=y_out,
        dst_ref=y_in,
        send_sem=y_send,
        recv_sem=y_recv,
        device_id={"member": m, "grid": (g + 1 + side * (GRID - 2)) % GRID},
        device_id_type=MESH,
    )

    def part_copy(c, i):
        peer = member_peer(i)
        return pltpu.make_async_remote_copy(
            src_ref=parts.at[peer["member"], rows_of(c)],
            dst_ref=xs.at[m, rows_of(c)],
            send_sem=part_send.at[c, i],
            recv_sem=part_recv.at[c, i],
            device_id=peer,
            device_id_type=MESH,
        )

    def own_copy(c):
        return pltpu.make_async_copy(
            parts.at[m, rows_of(c)], xs.at[m, rows_of(c)], own_sem.at[c]
        )

    def align(n):
        for k in range(GROUPS):
            before, left, right, after = aligned(xin[k, n])
            edge_out[k, n] = after
            edge_out[GROUPS + k, n] = before
            parts[k, n] = left
            parts[GROUPS + k, n] = right

    def send_edges(c):
        x_load(c).wait()
        repeat(run, lambda n: align(c * run + n))

        @pl.when(c == 0)
        def _():
            pl.semaphore_wait(barrier, len(meet))

        for s in range(2):
            edge_copy(c, s).start()

    repeat(CHUNKS, send_edges)
    y_load.wait()
    w_load.wait()
    full = rows // 8 * 8
    spread = y_rows.shape[0] // tiles

    def turn(t):
        cols = pl.ds(pl.multiple_of(t * LANES, LANES), LANES)
        for n in range(0, spread, 8):
            r = pl.multiple_of(jnp.minimum(row0 - group + n, full - 8), 8)
            value = yin[pl.ds(r, 8), cols]
            if n + 8 == spread:
                rest = jnp.zeros((8 + full - rows, LANES), F32)
                tail = jnp.concatenate([yin[pl.ds(full, rows - full), cols], rest], axis=0)
                value = jnp.where(group == GROUPS - 1, tail, value)
            y_rows[pl.ds(n * tiles + t, 8, stride=tiles), :] = value

    repeat(tiles, turn)

    def put_truth(n, row):
        before, left, right, after = aligned(row)
        y_out[n] = jnp.where(side == 0, after, before)
        y_own[n] = jnp.where(side == 0, left, right)

    def align_truth(n):
        put_truth(n, y_rows[pl.ds(pl.multiple_of((group + n) * tiles, tiles), tiles), :])

    repeat(share, align_truth)
    put_truth(share, win[...])
    y_copy.start()

    def owned(s):
        cell = s * edge + sub * LANES + lane
        return (cell >= lo_cell) & (cell < hi_cell)

    in_half = [owned(0), owned(1)]

    def send_parts(c):
        for s in range(2):
            edge_copy(c, s).wait_recv()

        def merge(n):
            for k in range(MEMBERS):
                parts[k, n] = jnp.where(in_half[k // GROUPS], parts[k, n], edge_in[k, n])

        repeat(run, lambda n: merge(c * run + n))
        for i in range(MEMBERS - 1):
            part_copy(c, i).start()
        own_copy(c).start()

    repeat(CHUNKS, send_parts)
    y_copy.wait_recv()
    in_own = owned(side)

    def merge_truth(n):
        y_own[n] = jnp.where(in_own, y_own[n], y_in[n])

    repeat(share + 1, merge_truth)
    own_area = y_own[share]

    def load_row(n):
        x = [xs[k, n] for k in range(MEMBERS)]
        y = y_own[n]
        return x, y, penalty[row0 + n] * own_area

    penalty_load.wait()

    def add(n, sums):
        sums = list(sums)
        x, y, lw = load_row(n)
        for k in range(MEMBERS):
            d = x[k] - y
            sums[k] = sums[k] + lw * d * d
        for e, (a, b) in enumerate(PAIRS):
            d = x[a] - x[b]
            sums[MEMBERS + e] = sums[MEMBERS + e] + lw * d * d
        return tuple(sums)

    def add_run(c, sums):
        own_copy(c).wait()
        for i in range(MEMBERS - 1):
            part_copy(c, i).wait_recv()
        return lax.fori_loop(c * run, c * run + run, add, sums)

    sums = lax.fori_loop(0, CHUNKS, add_run, (jnp.zeros((8, LANES), F32),) * ENTRIES)

    message = jnp.zeros((8, LANES), F32)
    for e in range(0, ENTRIES, 8):
        column = [jnp.sum(s, axis=0, keepdims=True) for s in sums[e : e + 8]]
        column += [jnp.zeros((1, LANES), F32)] * (8 - len(column))
        total = jnp.sum(jnp.concatenate(column, axis=0), axis=1, keepdims=True)
        message = jnp.where(lane == e // 8, total, message)

    def exchange(message, buffer, send, recv, peer_of, place):
        count = buffer.shape[0]
        buffer[place] = message

        def copy(i):
            return pltpu.make_async_remote_copy(
                src_ref=buffer.at[place],
                dst_ref=buffer.at[place],
                send_sem=send.at[i],
                recv_sem=recv.at[i],
                device_id=peer_of(i),
                device_id_type=MESH,
            )

        for i in range(count - 1):
            copy(i).start()
        for i in range(count - 1):
            copy(i).wait_recv()
        total = buffer[0]
        for i in range(1, count):
            total = total + buffer[i]
        return total, copy

    message, first_copy = exchange(
        message, first, first_send, first_recv, first_peer, my * NX + gx
    )
    message, second_copy = exchange(
        message, second, second_send, second_recv, second_peer, gz * NC + mc
    )

    scale = 1.0 / (rows * half * GRID)
    distance = jnp.sqrt(message * scale + 1e-06)
    entry = lane * 8 + sub
    is_truth = entry < MEMBERS
    share_of = jnp.where(is_truth, 1.0 / MEMBERS, -1.0 / (MEMBERS * (MEMBERS - 1)))
    loss[...] = jnp.sum(jnp.where(entry < ENTRIES, distance * share_of, 0.0), keepdims=True)
    loss_copy = pltpu.make_async_copy(loss, loss_out, loss_sem)
    loss_copy.start()
    factor = jnp.where(is_truth, 1.0, 1.0 / (MEMBERS - 1)) / distance
    for e in range(ENTRIES):
        coef[e] = jnp.broadcast_to(factor[e % 8 : e % 8 + 1, e // 8 : e // 8 + 1], (8, LANES))

    back = share // RETURNS

    def back_rows(c):
        return pl.ds(c * back, back)

    def place_of(c):
        return out.at[pl.ds(row0 + c * back, back), pl.ds(pl.multiple_of(side * 8, 8), 8)]

    def res_copy(c, i):
        peer = member_peer(i)
        return pltpu.make_async_remote_copy(
            src_ref=result.at[peer["member"], back_rows(c)],
            dst_ref=place_of(c),
            send_sem=res_send.at[c, i],
            recv_sem=res_recv.at[c, i],
            device_id=peer,
            device_id_type=MESH,
        )

    def keep_copy(c):
        return pltpu.make_async_copy(result.at[m, back_rows(c)], place_of(c), keep_sem.at[c])

    def derive(n):
        x, y, lw = load_row(n)
        o = [(x[k] - y) * coef[k] for k in range(MEMBERS)]
        for e, (a, b) in enumerate(PAIRS):
            d = (x[a] - x[b]) * coef[MEMBERS + e]
            o[a] = o[a] - d
            o[b] = o[b] + d
        for k in range(MEMBERS):
            result[k, n] = lw * o[k]

    def send_back(c):
        repeat(back, lambda n: derive(c * back + n))
        for i in range(MEMBERS - 1):
            res_copy(c, i).start()
        keep_copy(c).start()

    repeat(RETURNS, send_back)

    def end_run(c):
        for s in range(2):
            edge_copy(c, s).wait_send()
        for i in range(MEMBERS - 1):
            part_copy(c, i).wait_send()

    repeat(CHUNKS, end_run)
    y_copy.wait_send()
    for i in range(NX * NY - 1):
        first_copy(i).wait_send()
    for i in range(NZ * NC - 1):
        second_copy(i).wait_send()
    loss_copy.wait()

    def end_back(c):
        keep_copy(c).wait()

        for i in range(MEMBERS - 1):
            res_copy(c, i).wait_send()
            res_copy(c, i).wait_recv()

    repeat(RETURNS, end_back)


def local(prediction, reference_state, penalty, area, starts):
    rows, slots = prediction.shape[1:]
    tiles = slots // LANES
    share = rows // GROUPS
    spread = -(-(share + GROUPS - 1) // 8) * 8
    vmem = functools.partial(pltpu.VMEM, dtype=F32)
    array = functools.partial(jax.ShapeDtypeStruct, dtype=F32)
    dma = pltpu.SemaphoreType.DMA
    anywhere = pl.BlockSpec(memory_space=pl.ANY)
    fields = (MEMBERS, share, 8, LANES)
    y_share = (share + 1, 8, LANES)
    result, loss = pl.pallas_call(
        kernel,
        name="energy_score",
        out_shape=(pltpu.VMEM((rows, tiles // 2, LANES), F32), array((1, 1))),
        in_specs=[anywhere] * 5,
        out_specs=(anywhere, anywhere),
        scratch_shapes=[
            pltpu.SMEM(starts.shape, jnp.int32),
            pltpu.SMEM(penalty.shape, F32),
            vmem((1, 1)),
            vmem((GROUPS, share, tiles, LANES)),
            vmem((rows, slots)),
            vmem((tiles, LANES)),
            vmem((spread * tiles, LANES)),
            vmem(fields),
            vmem(fields),
            vmem(fields),
            vmem(fields),
            vmem(y_share),
            vmem(y_share),
            vmem(y_share),
            vmem(fields),
            vmem((NX * NY, 8, LANES)),
            vmem((NZ * NC, 8, LANES)),
            vmem((ENTRIES, 8, LANES)),
            dma((CHUNKS + 4,)),
            dma((CHUNKS, 2)),
            dma((CHUNKS, 2)),
            dma,
            dma,
            dma((CHUNKS, MEMBERS - 1)),
            dma((CHUNKS, MEMBERS - 1)),
            dma((CHUNKS,)),
            dma((NX * NY - 1,)),
            dma((NX * NY - 1,)),
            dma((NZ * NC - 1,)),
            dma((NZ * NC - 1,)),
            dma((RETURNS, MEMBERS - 1)),
            dma((RETURNS, MEMBERS - 1)),
            dma((RETURNS,)),
            dma,
        ],
        compiler_params=pltpu.CompilerParams(
            collective_id=0, has_side_effects=True, vmem_limit_bytes=VMEM_BYTES
        ),
    )(
        starts,
        penalty,
        prediction.reshape(GROUPS, share, tiles, LANES),
        reference_state,
        area.reshape(tiles, LANES),
    )
    return (result.reshape(1, rows, slots // 2), loss.reshape(()))


def solution(mesh):
    placed = (P("member", None, "grid"), P(None, "grid"), P(), P("grid"), P())
    return jax.shard_map(
        local,
        mesh=mesh,
        in_specs=placed,
        out_specs=(P("member", None, "grid"), P()),
        check_vma=False,
    )
```

time: 54.2 us -> 52.9 us (0.976)
  Pallas kernels: 50.9 us -> 49.6 us
    pallas_call x1, Pallas kernels: 50.9 us -> 49.6 us  [local(): pl.pallas_call(kernel, name='energy_score', out_shape=(pltpu.VMEM((rows,...]
where the time goes in v4:
time: 52.9 us; the launch traced here: 52.8 us
  Pallas kernels  49.6 us (94%)
  between operations  2.33 us (4%)
  local copies, waits for them, and re-layouts  0.89 us (2%)
    pallas_call x1, Pallas kernels, local(): pl.pallas_call(kernel, name='energy_score', out_shape=(pltpu.VMEM((rows,...  49.6 us

profile of v4, /device:TPU:1, one launch (start us, length us, event | category | flops | bytes accessed | tf_op | source)
XLA Modules:
  0.0 52.8 jit_solution(8393620446571991177)
XLA Ops:
  0.6 49.6 %energy_score.1 = (f32[100,16,128]{2,1,0:T(8,128)S(1)}, f32[1,1]{1,0:T(1,128)}) custom-call(s32[33]{0:T(128)} %starts_in.1, f32[100]{0:T(128)} %penalty_in.1, f32[4,25,32,128]{3,2,1,0:T(8,128)} %bitcast.5, f32[100,4096]{1,0:T(8,128)} %truth.1, f32[32,128]{1,0:T(8,128)} %bitcast.6), custom_call_target="tpu_custom_call" | custom-call | tf_op jit(solution)/shard_map/energy_score/pallas_call | solution.py:429
  50.2 0.9 %copy.11 = f32[1,100,2048]{2,0,1:T(1,128)} copy(f32[1,100,2048]{2,0,1:T(1,128)S(1)} %bitcast.4) | data formatting | bytes 1638400

commit v5 on v4

--- a/solution.py
+++ b/solution.py
@@ -11,13 +11,14 @@
 F32 = jnp.float32
 LANES = 128
 VMEM_BYTES = 56 * 2**20
-CHUNKS = 5
+CHUNKS = ((0, 5), (5, 10), (10, 15), (15, 20), (20, 25))
 RETURNS = 5
 NX, NZ = 4, 8
 NY, NC = 4, 2
 MEMBERS = 8
 GRID = 32
-GROUPS = MEMBERS // 2
+SIDES = 2
+GROUPS = MEMBERS // SIDES
 PAIRS = [(a, b) for a in range(MEMBERS) for b in range(a + 1, MEMBERS)]
 ENTRIES = MEMBERS + len(PAIRS)
 
@@ -37,12 +38,16 @@
 )
 
 
-def repeat(count, body):
+def repeat(first, end, body):
     def step(i, carry):
         body(i)
         return carry
 
-    lax.fori_loop(0, count, step, 0)
+    lax.fori_loop(first, end, step, 0)
+
+
+def wait_for(ref, sem):
+    pltpu.make_async_copy(ref, ref, sem).wait()
 
 
 def kernel(
@@ -78,26 +83,23 @@
     y_recv,
     part_send,
     part_recv,
-    own_sem,
     first_send,
     first_recv,
     second_send,
     second_recv,
     res_send,
     res_recv,
-    keep_sem,
     loss_sem,
 ):
     share, tiles = pred.shape[1], pred.shape[2]
     rows = share * GROUPS
     edge = tiles // 4 * LANES
     half = 2 * edge
-    run = share // CHUNKS
     m = lax.axis_index("member")
     g = lax.axis_index("grid")
     my, mc = m // NC, m % NC
     gx, gz = g // NZ, g % NZ
-    side, group = m // GROUPS, m % GROUPS
+    side, group = m % SIDES, m // SIDES
     row0 = group * share
 
     def moved(z=0, y=0, x=0, core=0):
@@ -129,19 +131,21 @@
         pl.semaphore_signal(barrier, inc=1, device_id=peer, device_id_type=MESH)
 
     def rows_of(c):
-        return pl.ds(c * run, run)
+        lo, hi = CHUNKS[c]
+        return pl.ds(lo, hi - lo)
 
     def x_load(c):
         return pltpu.make_async_copy(
             pred.at[:, rows_of(c)], xin.at[:, rows_of(c)], load_sem.at[c]
         )
 
-    y_load = pltpu.make_async_copy(truth, yin, load_sem.at[CHUNKS])
-    w_load = pltpu.make_async_copy(area, win, load_sem.at[CHUNKS + 1])
-    starts_load = pltpu.make_async_copy(starts_in, starts, load_sem.at[CHUNKS + 2])
-    penalty_load = pltpu.make_async_copy(penalty_in, penalty, load_sem.at[CHUNKS + 3])
+    y_load = pltpu.make_async_copy(truth, yin, load_sem.at[len(CHUNKS)])
+    w_load = pltpu.make_async_copy(area, win, load_sem.at[len(CHUNKS) + 1])
+    starts_load = pltpu.make_async_copy(starts_in, starts, load_sem.at[len(CHUNKS) + 2])
+    penalty_load = pltpu.make_async_copy(penalty_in, penalty, load_sem.at[len(CHUNKS) + 3])
     starts_load.start()
-    repeat(CHUNKS, lambda c: x_load(c).start())
+    for c in range(len(CHUNKS)):
+        x_load(c).start()
     for copy in (y_load, w_load, penalty_load):
         copy.start()
 
@@ -162,12 +166,12 @@
     sub = lax.broadcasted_iota(jnp.int32, (8, LANES), 0)
 
     def edge_copy(c, s):
-        where = (pl.ds(s * GROUPS, GROUPS), rows_of(c))
+        where = (s, slice(None), rows_of(c))
         return pltpu.make_async_remote_copy(
             src_ref=edge_out.at[where],
             dst_ref=edge_in.at[where],
-            send_sem=edge_send.at[c, s],
-            recv_sem=edge_recv.at[c, s],
+            send_sem=edge_send,
+            recv_sem=edge_recv.at[c],
             device_id=grid_peer(1 if s == 0 else -1),
             device_id_type=MESH,
         )
@@ -186,37 +190,38 @@
         return pltpu.make_async_remote_copy(
             src_ref=parts.at[peer["member"], rows_of(c)],
             dst_ref=xs.at[m, rows_of(c)],
-            send_sem=part_send.at[c, i],
-            recv_sem=part_recv.at[c, i],
+            send_sem=part_send,
+            recv_sem=part_recv.at[c],
             device_id=peer,
             device_id_type=MESH,
         )
 
     def own_copy(c):
         return pltpu.make_async_copy(
-            parts.at[m, rows_of(c)], xs.at[m, rows_of(c)], own_sem.at[c]
+            parts.at[m, rows_of(c)], xs.at[m, rows_of(c)], part_recv.at[c]
         )
+
+    def send_parts(c):
+        for i in range(MEMBERS - 1):
+            part_copy(c, i).start()
+        own_copy(c).start()
 
     def align(n):
         for k in range(GROUPS):
             before, left, right, after = aligned(xin[k, n])
-            edge_out[k, n] = after
-            edge_out[GROUPS + k, n] = before
-            parts[k, n] = left
-            parts[GROUPS + k, n] = right
-
-    def send_edges(c):
+            edge_out[0, k, n] = after
+            edge_out[1, k, n] = before
+            parts[SIDES * k, n] = left
+            parts[SIDES * k + 1, n] = right
+
+    for c, (lo, hi) in enumerate(CHUNKS):
         x_load(c).wait()
-        repeat(run, lambda n: align(c * run + n))
-
-        @pl.when(c == 0)
-        def _():
+        repeat(lo, hi, align)
+        if c == 0:
             pl.semaphore_wait(barrier, len(meet))
-
-        for s in range(2):
+        for s in range(SIDES):
             edge_copy(c, s).start()
 
-    repeat(CHUNKS, send_edges)
     y_load.wait()
     w_load.wait()
     full = rows // 8 * 8
@@ -233,7 +238,7 @@
                 value = jnp.where(group == GROUPS - 1, tail, value)
             y_rows[pl.ds(n * tiles + t, 8, stride=tiles), :] = value
 
-    repeat(tiles, turn)
+    repeat(0, tiles, turn)
 
     def put_truth(n, row):
         before, left, right, after = aligned(row)
@@ -243,7 +248,7 @@
     def align_truth(n):
         put_truth(n, y_rows[pl.ds(pl.multiple_of((group + n) * tiles, tiles), tiles), :])
 
-    repeat(share, align_truth)
+    repeat(0, share, align_truth)
     put_truth(share, win[...])
     y_copy.start()
 
@@ -253,27 +258,23 @@
 
     in_half = [owned(0), owned(1)]
 
-    def send_parts(c):
-        for s in range(2):
-            edge_copy(c, s).wait_recv()
-
-        def merge(n):
-            for k in range(MEMBERS):
-                parts[k, n] = jnp.where(in_half[k // GROUPS], parts[k, n], edge_in[k, n])
-
-        repeat(run, lambda n: merge(c * run + n))
-        for i in range(MEMBERS - 1):
-            part_copy(c, i).start()
-        own_copy(c).start()
-
-    repeat(CHUNKS, send_parts)
+    def merge(n):
+        for k in range(MEMBERS):
+            s = k % SIDES
+            parts[k, n] = jnp.where(in_half[s], parts[k, n], edge_in[s, k // SIDES, n])
+
+    for c, (lo, hi) in enumerate(CHUNKS):
+        wait_for(edge_in.at[:, :, rows_of(c)], edge_recv.at[c])
+        repeat(lo, hi, merge)
+        send_parts(c)
+
     y_copy.wait_recv()
     in_own = owned(side)
 
     def merge_truth(n):
         y_own[n] = jnp.where(in_own, y_own[n], y_in[n])
 
-    repeat(share + 1, merge_truth)
+    repeat(0, share + 1, merge_truth)
     own_area = y_own[share]
 
     def load_row(n):
@@ -294,13 +295,10 @@
             sums[MEMBERS + e] = sums[MEMBERS + e] + lw * d * d
         return tuple(sums)
 
-    def add_run(c, sums):
-        own_copy(c).wait()
-        for i in range(MEMBERS - 1):
-            part_copy(c, i).wait_recv()
-        return lax.fori_loop(c * run, c * run + run, add, sums)
-
-    sums = lax.fori_loop(0, CHUNKS, add_run, (jnp.zeros((8, LANES), F32),) * ENTRIES)
+    sums = (jnp.zeros((8, LANES), F32),) * ENTRIES
+    for c, (lo, hi) in enumerate(CHUNKS):
+        wait_for(xs.at[:, rows_of(c)], part_recv.at[c])
+        sums = lax.fori_loop(lo, hi, add, sums)
 
     message = jnp.zeros((8, LANES), F32)
     for e in range(0, ENTRIES, 8):
@@ -313,29 +311,25 @@
         count = buffer.shape[0]
         buffer[place] = message
 
-        def copy(i):
-            return pltpu.make_async_remote_copy(
+        for i in range(count - 1):
+            pltpu.make_async_remote_copy(
                 src_ref=buffer.at[place],
                 dst_ref=buffer.at[place],
-                send_sem=send.at[i],
-                recv_sem=recv.at[i],
+                send_sem=send,
+                recv_sem=recv,
                 device_id=peer_of(i),
                 device_id_type=MESH,
-            )
-
-        for i in range(count - 1):
-            copy(i).start()
-        for i in range(count - 1):
-            copy(i).wait_recv()
+            ).start()
+        wait_for(buffer.at[pl.ds(0, count - 1)], recv)
         total = buffer[0]
         for i in range(1, count):
             total = total + buffer[i]
-        return total, copy
-
-    message, first_copy = exchange(
+        return total
+
+    message = exchange(
         message, first, first_send, first_recv, first_peer, my * NX + gx
     )
-    message, second_copy = exchange(
+    message = exchange(
         message, second, second_send, second_recv, second_peer, gz * NC + mc
     )
 
@@ -364,14 +358,14 @@
         return pltpu.make_async_remote_copy(
             src_ref=result.at[peer["member"], back_rows(c)],
             dst_ref=place_of(c),
-            send_sem=res_send.at[c, i],
-            recv_sem=res_recv.at[c, i],
+            send_sem=res_send,
+            recv_sem=res_recv,
             device_id=peer,
             device_id_type=MESH,
         )
 
     def keep_copy(c):
-        return pltpu.make_async_copy(result.at[m, back_rows(c)], place_of(c), keep_sem.at[c])
+        return pltpu.make_async_copy(result.at[m, back_rows(c)], place_of(c), res_recv)
 
     def derive(n):
         x, y, lw = load_row(n)
@@ -384,35 +378,21 @@
             result[k, n] = lw * o[k]
 
     def send_back(c):
-        repeat(back, lambda n: derive(c * back + n))
+        repeat(c * back, c * back + back, derive)
         for i in range(MEMBERS - 1):
             res_copy(c, i).start()
         keep_copy(c).start()
 
-    repeat(RETURNS, send_back)
-
-    def end_run(c):
-        for s in range(2):
-            edge_copy(c, s).wait_send()
-        for i in range(MEMBERS - 1):
-            part_copy(c, i).wait_send()
-
-    repeat(CHUNKS, end_run)
+    repeat(0, RETURNS, send_back)
+
+    wait_for(edge_out, edge_send)
+    wait_for(parts.at[pl.ds(0, MEMBERS - 1)], part_send)
     y_copy.wait_send()
-    for i in range(NX * NY - 1):
-        first_copy(i).wait_send()
-    for i in range(NZ * NC - 1):
-        second_copy(i).wait_send()
+    wait_for(first.at[pl.ds(0, NX * NY - 1)], first_send)
+    wait_for(second.at[pl.ds(0, NZ * NC - 1)], second_send)
     loss_copy.wait()
-
-    def end_back(c):
-        keep_copy(c).wait()
-
-        for i in range(MEMBERS - 1):
-            res_copy(c, i).wait_send()
-            res_copy(c, i).wait_recv()
-
-    repeat(RETURNS, end_back)
+    wait_for(result.at[pl.ds(0, MEMBERS - 1)], res_send)
+    wait_for(out, res_recv)
 
 
 def local(prediction, reference_state, penalty, area, starts):
@@ -425,6 +405,8 @@
     dma = pltpu.SemaphoreType.DMA
     anywhere = pl.BlockSpec(memory_space=pl.ANY)
     fields = (MEMBERS, share, 8, LANES)
+    edges = (SIDES, GROUPS, share, 8, LANES)
+    runs = len(CHUNKS)
     y_share = (share + 1, 8, LANES)
     result, loss = pl.pallas_call(
         kernel,
@@ -440,8 +422,8 @@
             vmem((rows, slots)),
             vmem((tiles, LANES)),
             vmem((spread * tiles, LANES)),
-            vmem(fields),
-            vmem(fields),
+            vmem(edges),
+            vmem(edges),
             vmem(fields),
             vmem(fields),
             vmem(y_share),
@@ -451,21 +433,19 @@
             vmem((NX * NY, 8, LANES)),
             vmem((NZ * NC, 8, LANES)),
             vmem((ENTRIES, 8, LANES)),
-            dma((CHUNKS + 4,)),
-            dma((CHUNKS, 2)),
-            dma((CHUNKS, 2)),
-            dma,
-            dma,
-            dma((CHUNKS, MEMBERS - 1)),
-            dma((CHUNKS, MEMBERS - 1)),
-            dma((CHUNKS,)),
-            dma((NX * NY - 1,)),
-            dma((NX * NY - 1,)),
-            dma((NZ * NC - 1,)),
-            dma((NZ * NC - 1,)),
-            dma((RETURNS, MEMBERS - 1)),
-            dma((RETURNS, MEMBERS - 1)),
-            dma((RETURNS,)),
+            dma((runs + 4,)),
+            dma,
+            dma((runs,)),
+            dma,
+            dma,
+            dma,
+            dma((runs,)),
+            dma,
+            dma,
+            dma,
+            dma,
+            dma,
+            dma,
             dma,
         ],
         compiler_params=pltpu.CompilerParams(

time: 52.9 us -> 50.9 us (0.962)
  Pallas kernels: 49.6 us -> 47.6 us
    pallas_call x1, Pallas kernels: 49.6 us -> 47.6 us  [local(): pl.pallas_call(kernel, name='energy_score', out_shape=(pltpu.VMEM((rows,...]
where the time goes in v5:
time: 50.9 us; the launch traced here: 50.8 us
  Pallas kernels  47.6 us (94%)
  between operations  2.33 us (5%)
  local copies, waits for them, and re-layouts  0.89 us (2%)
    pallas_call x1, Pallas kernels, local(): pl.pallas_call(kernel, name='energy_score', out_shape=(pltpu.VMEM((rows,...  47.6 us

profile of v5, /device:TPU:1, one launch (start us, length us, event | category | flops | bytes accessed | tf_op | source)
XLA Modules:
  0.0 50.8 jit_solution(15282675059572672433)
XLA Ops:
  0.6 47.6 %energy_score.1 = (f32[100,16,128]{2,1,0:T(8,128)S(1)}, f32[1,1]{1,0:T(1,128)}) custom-call(s32[33]{0:T(128)} %starts_in.1, f32[100]{0:T(128)} %penalty_in.1, f32[4,25,32,128]{3,2,1,0:T(8,128)} %bitcast.5, f32[100,4096]{1,0:T(8,128)} %truth.1, f32[32,128]{1,0:T(8,128)} %bitcast.6), custom_call_target="tpu_custom_call" | custom-call | tf_op jit(solution)/shard_map/energy_score/pallas_call | solution.py:411
  48.2 0.9 %copy.11 = f32[1,100,2048]{2,0,1:T(1,128)} copy(f32[1,100,2048]{2,0,1:T(1,128)S(1)} %bitcast.4) | data formatting | bytes 1638400

commit v6 on v5

--- a/solution.py
+++ b/solution.py
@@ -1,4 +1,6 @@
 import functools
+import itertools
+import math
 
 import jax
 import jax.numpy as jnp
@@ -11,7 +13,7 @@
 F32 = jnp.float32
 LANES = 128
 VMEM_BYTES = 56 * 2**20
-CHUNKS = ((0, 5), (5, 10), (10, 15), (15, 20), (20, 25))
+CHUNKS = ((0, 3), (3, 7), (7, 11), (11, 15), (15, 19), (19, 22), (22, 25))
 RETURNS = 5
 NX, NZ = 4, 8
 NY, NC = 4, 2
@@ -23,19 +25,24 @@
 ENTRIES = MEMBERS + len(PAIRS)
 
 
-def ring(step, count):
-    return min(step, count - step)
+AXES = {"z": NZ, "y": NY, "x": NX, "core": NC}
+STAGES = (("z", "core"), ("y", "x"))
+
+
+def hops(step):
+    return sum(min(step[a], AXES[a] - step[a]) for a in step)
+
+
+def steps(axes):
+    ways = itertools.product(*(range(AXES[a]) for a in axes))
+    ways = [dict(zip(axes, way)) for way in ways if any(way)]
+    return sorted(ways, key=lambda way: -hops(way))
 
 
 MEMBER_STEPS = ((0, 1), (2, 0), (1, 0), (3, 0), (2, 1), (1, 1), (3, 1))
-FIRST_STEPS = sorted(
-    [(y, x) for y in range(NY) for x in range(NX) if y or x],
-    key=lambda s: -ring(s[0], NY) - ring(s[1], NX),
-)
-SECOND_STEPS = sorted(
-    [(z, core) for z in range(NZ) for core in range(NC) if z or core],
-    key=lambda s: (-ring(s[0], NZ), -s[1]),
-)
+MEET = [dict(y=y, core=core) for y, core in MEMBER_STEPS]
+for axes in STAGES:
+    MEET += [way for way in steps(axes) if set(k for k in way if way[k]) - {"y", "core"}]
 
 
 def repeat(first, end, body):
@@ -114,17 +121,8 @@
     def grid_peer(step):
         return {"member": m, "grid": (g + step + GRID) % GRID}
 
-    def first_peer(i):
-        y, x = FIRST_STEPS[i]
-        return moved(y=y, x=x)
-
-    def second_peer(i):
-        z, core = SECOND_STEPS[i]
-        return moved(z=z, core=core)
-
-    meet = [(ring(z, NZ), moved(z=z, core=core)) for z, core in SECOND_STEPS if z]
-    meet += [(ring(y, NY) + ring(x, NX), moved(y=y, x=x)) for y, x in FIRST_STEPS if x]
-    meet += [(ring(y, NY), moved(y=y, core=core)) for y, core in MEMBER_STEPS]
+    here = {"z": gz, "y": my, "x": gx, "core": mc}
+    meet = [(hops(way), moved(**way)) for way in MEET]
     meet += [(2, grid_peer(1)), (2, grid_peer(-1))]
     barrier = pltpu.get_barrier_semaphore()
     for _, peer in sorted(meet, key=lambda entry: -entry[0]):
@@ -307,17 +305,17 @@
         total = jnp.sum(jnp.concatenate(column, axis=0), axis=1, keepdims=True)
         message = jnp.where(lane == e // 8, total, message)
 
-    def exchange(message, buffer, send, recv, peer_of, place):
+    def add_over(axes, message, buffer, send, recv):
+        place = functools.reduce(lambda at, a: at * AXES[a] + here[a], axes, 0)
+        buffer[place] = message
         count = buffer.shape[0]
-        buffer[place] = message
-
-        for i in range(count - 1):
+        for way in steps(axes):
             pltpu.make_async_remote_copy(
                 src_ref=buffer.at[place],
                 dst_ref=buffer.at[place],
                 send_sem=send,
                 recv_sem=recv,
-                device_id=peer_of(i),
+                device_id=moved(**way),
                 device_id_type=MESH,
             ).start()
         wait_for(buffer.at[pl.ds(0, count - 1)], recv)
@@ -326,12 +324,8 @@
             total = total + buffer[i]
         return total
 
-    message = exchange(
-        message, first, first_send, first_recv, first_peer, my * NX + gx
-    )
-    message = exchange(
-        message, second, second_send, second_recv, second_peer, gz * NC + mc
-    )
+    message = add_over(STAGES[0], message, first, first_send, first_recv)
+    message = add_over(STAGES[1], message, second, second_send, second_recv)
 
     scale = 1.0 / (rows * half * GRID)
     distance = jnp.sqrt(message * scale + 1e-06)
@@ -388,8 +382,8 @@
     wait_for(edge_out, edge_send)
     wait_for(parts.at[pl.ds(0, MEMBERS - 1)], part_send)
     y_copy.wait_send()
-    wait_for(first.at[pl.ds(0, NX * NY - 1)], first_send)
-    wait_for(second.at[pl.ds(0, NZ * NC - 1)], second_send)
+    wait_for(first.at[pl.ds(0, first.shape[0] - 1)], first_send)
+    wait_for(second.at[pl.ds(0, second.shape[0] - 1)], second_send)
     loss_copy.wait()
     wait_for(result.at[pl.ds(0, MEMBERS - 1)], res_send)
     wait_for(out, res_recv)
@@ -430,8 +424,8 @@
             vmem(y_share),
             vmem(y_share),
             vmem(fields),
-            vmem((NX * NY, 8, LANES)),
-            vmem((NZ * NC, 8, LANES)),
+            vmem((math.prod(AXES[a] for a in STAGES[0]), 8, LANES)),
+            vmem((math.prod(AXES[a] for a in STAGES[1]), 8, LANES)),
             vmem((ENTRIES, 8, LANES)),
             dma((runs + 4,)),
             dma,

time: 50.9 us -> 49.8 us (0.978)
  Pallas kernels: 47.6 us -> 46.5 us
    pallas_call x1, Pallas kernels: 47.6 us -> 46.5 us  [local(): pl.pallas_call(kernel, name='energy_score', out_shape=(pltpu.VMEM((rows,...]
where the time goes in v6:
time: 49.8 us; the launch traced here: 49.7 us
  Pallas kernels  46.5 us (93%)
  between operations  2.33 us (5%)
  local copies, waits for them, and re-layouts  0.89 us (2%)
    pallas_call x1, Pallas kernels, local(): pl.pallas_call(kernel, name='energy_score', out_shape=(pltpu.VMEM((rows,...  46.5 us

profile of v6, /device:TPU:1, one launch (start us, length us, event | category | flops | bytes accessed | tf_op | source)
XLA Modules:
  0.0 49.7 jit_solution(200464360731835480)
XLA Ops:
  0.6 46.5 %energy_score.1 = (f32[100,16,128]{2,1,0:T(8,128)S(1)}, f32[1,1]{1,0:T(1,128)}) custom-call(s32[33]{0:T(128)} %starts_in.1, f32[100]{0:T(128)} %penalty_in.1, f32[4,25,32,128]{3,2,1,0:T(8,128)} %bitcast.5, f32[100,4096]{1,0:T(8,128)} %truth.1, f32[32,128]{1,0:T(8,128)} %bitcast.6), custom_call_target="tpu_custom_call" | custom-call | tf_op jit(solution)/shard_map/energy_score/pallas_call | solution.py:405
  47.1 0.9 %copy.11 = f32[1,100,2048]{2,0,1:T(1,128)} copy(f32[1,100,2048]{2,0,1:T(1,128)S(1)} %bitcast.4) | data formatting | bytes 1638400

commit v7 on v6

--- a/solution.py
+++ b/solution.py
@@ -223,7 +223,7 @@
     y_load.wait()
     w_load.wait()
     full = rows // 8 * 8
-    spread = y_rows.shape[0] // tiles
+    spread = y_rows.shape[0] // tiles - 1
 
     def turn(t):
         cols = pl.ds(pl.multiple_of(t * LANES, LANES), LANES)
@@ -415,7 +415,7 @@
             vmem((GROUPS, share, tiles, LANES)),
             vmem((rows, slots)),
             vmem((tiles, LANES)),
-            vmem((spread * tiles, LANES)),
+            vmem(((spread + 1) * tiles, LANES)),
             vmem(edges),
             vmem(edges),
             vmem(fields),

time: 49.8 us -> 49.8 us (level)
  no operation moved by 1% of the time
where the time goes in v7:
time: 49.8 us; the launch traced here: 49.7 us
  Pallas kernels  46.5 us (93%)
  between operations  2.33 us (5%)
  local copies, waits for them, and re-layouts  0.89 us (2%)
    pallas_call x1, Pallas kernels, local(): pl.pallas_call(kernel, name='energy_score', out_shape=(pltpu.VMEM((rows,...  46.5 us

profile of v7, /device:TPU:1, one launch (start us, length us, event | category | flops | bytes accessed | tf_op | source)
XLA Modules:
  0.0 49.7 jit_solution(7231941434545621902)
XLA Ops:
  0.6 46.5 %energy_score.1 = (f32[100,16,128]{2,1,0:T(8,128)S(1)}, f32[1,1]{1,0:T(1,128)}) custom-call(s32[33]{0:T(128)} %starts_in.1, f32[100]{0:T(128)} %penalty_in.1, f32[4,25,32,128]{3,2,1,0:T(8,128)} %bitcast.5, f32[100,4096]{1,0:T(8,128)} %truth.1, f32[32,128]{1,0:T(8,128)} %bitcast.6), custom_call_target="tpu_custom_call" | custom-call | tf_op jit(solution)/shard_map/energy_score/pallas_call | solution.py:405
  47.1 0.9 %copy.11 = f32[1,100,2048]{2,0,1:T(1,128)} copy(f32[1,100,2048]{2,0,1:T(1,128)S(1)} %bitcast.4) | data formatting | bytes 1638400

commit v8 on v7

--- a/solution.py
+++ b/solution.py
@@ -41,8 +41,9 @@
 
 MEMBER_STEPS = ((0, 1), (2, 0), (1, 0), (3, 0), (2, 1), (1, 1), (3, 1))
 MEET = [dict(y=y, core=core) for y, core in MEMBER_STEPS]
-for axes in STAGES:
-    MEET += [way for way in steps(axes) if set(k for k in way if way[k]) - {"y", "core"}]
+MEET += [dict(x=x) for x in range(1, NX)] + [dict(z=1), dict(z=NZ - 1)]
+RELAY_AFTER = (1, 3, 6)
+RELAYS = NZ // 2 - 1
 
 
 def repeat(first, end, body):
@@ -97,6 +98,7 @@
     res_send,
     res_recv,
     loss_sem,
+    relay,
 ):
     share, tiles = pred.shape[1], pred.shape[2]
     rows = share * GROUPS
@@ -128,6 +130,10 @@
     for _, peer in sorted(meet, key=lambda entry: -entry[0]):
         pl.semaphore_signal(barrier, inc=1, device_id=peer, device_id_type=MESH)
 
+    def pass_on(i):
+        for z in (1, NZ - 1):
+            pl.semaphore_signal(relay.at[i], inc=1, device_id=moved(z=z), device_id_type=MESH)
+
     def rows_of(c):
         lo, hi = CHUNKS[c]
         return pl.ds(lo, hi - lo)
@@ -217,6 +223,7 @@
         repeat(lo, hi, align)
         if c == 0:
             pl.semaphore_wait(barrier, len(meet))
+            pass_on(0)
         for s in range(SIDES):
             edge_copy(c, s).start()
 
@@ -264,6 +271,11 @@
     for c, (lo, hi) in enumerate(CHUNKS):
         wait_for(edge_in.at[:, :, rows_of(c)], edge_recv.at[c])
         repeat(lo, hi, merge)
+        if c in RELAY_AFTER:
+            i = RELAY_AFTER.index(c)
+            pl.semaphore_wait(relay.at[i], 2)
+            if i + 1 < RELAYS:
+                pass_on(i + 1)
         send_parts(c)
 
     y_copy.wait_recv()
@@ -441,6 +453,7 @@
             dma,
             dma,
             dma,
+            pltpu.SemaphoreType.REGULAR((RELAYS,)),
         ],
         compiler_params=pltpu.CompilerParams(
             collective_id=0, has_side_effects=True, vmem_limit_bytes=VMEM_BYTES

time: 49.8 us -> 49.4 us (level)
  no operation moved by 1% of the time
where the time goes in v8:
time: 49.4 us; the launch traced here: 49.3 us
  Pallas kernels  46.1 us (93%)
  between operations  2.33 us (5%)
  local copies, waits for them, and re-layouts  0.89 us (2%)
    pallas_call x1, Pallas kernels, local(): pl.pallas_call(kernel, name='energy_score', out_shape=(pltpu.VMEM((rows,...  46.1 us

profile of v8, /device:TPU:1, one launch (start us, length us, event | category | flops | bytes accessed | tf_op | source)
XLA Modules:
  0.0 49.3 jit_solution(15450784615376295024)
XLA Ops:
  0.6 46.1 %energy_score.1 = (f32[100,16,128]{2,1,0:T(8,128)S(1)}, f32[1,1]{1,0:T(1,128)}) custom-call(s32[33]{0:T(128)} %starts_in.1, f32[100]{0:T(128)} %penalty_in.1, f32[4,25,32,128]{3,2,1,0:T(8,128)} %bitcast.5, f32[100,4096]{1,0:T(8,128)} %truth.1, f32[32,128]{1,0:T(8,128)} %bitcast.6), custom_call_target="tpu_custom_call" | custom-call | tf_op jit(solution)/shard_map/energy_score/pallas_call | solution.py:417
  46.7 0.9 %copy.11 = f32[1,100,2048]{2,0,1:T(1,128)} copy(f32[1,100,2048]{2,0,1:T(1,128)S(1)} %bitcast.4) | data formatting | bytes 1638400

commit v9 on v8

--- a/solution.py
+++ b/solution.py
@@ -315,7 +315,8 @@
         column = [jnp.sum(s, axis=0, keepdims=True) for s in sums[e : e + 8]]
         column += [jnp.zeros((1, LANES), F32)] * (8 - len(column))
         total = jnp.sum(jnp.concatenate(column, axis=0), axis=1, keepdims=True)
-        message = jnp.where(lane == e // 8, total, message)
+        message = jnp.where(lane == e + sub, total, message)
+    message = jnp.sum(message, axis=0, keepdims=True)
 
     def add_over(axes, message, buffer, send, recv):
         place = functools.reduce(lambda at, a: at * AXES[a] + here[a], axes, 0)
@@ -341,7 +342,7 @@
 
     scale = 1.0 / (rows * half * GRID)
     distance = jnp.sqrt(message * scale + 1e-06)
-    entry = lane * 8 + sub
+    entry = lane[:1]
     is_truth = entry < MEMBERS
     share_of = jnp.where(is_truth, 1.0 / MEMBERS, -1.0 / (MEMBERS * (MEMBERS - 1)))
     loss[...] = jnp.sum(jnp.where(entry < ENTRIES, distance * share_of, 0.0), keepdims=True)
@@ -349,7 +350,7 @@
     loss_copy.start()
     factor = jnp.where(is_truth, 1.0, 1.0 / (MEMBERS - 1)) / distance
     for e in range(ENTRIES):
-        coef[e] = jnp.broadcast_to(factor[e % 8 : e % 8 + 1, e // 8 : e // 8 + 1], (8, LANES))
+        coef[e] = jnp.broadcast_to(factor[:, e : e + 1], (8, LANES))
 
     back = share // RETURNS
 
@@ -436,8 +437,8 @@
             vmem(y_share),
             vmem(y_share),
             vmem(fields),
-            vmem((math.prod(AXES[a] for a in STAGES[0]), 8, LANES)),
-            vmem((math.prod(AXES[a] for a in STAGES[1]), 8, LANES)),
+            vmem((math.prod(AXES[a] for a in STAGES[0]), 1, LANES)),
+            vmem((math.prod(AXES[a] for a in STAGES[1]), 1, LANES)),
             vmem((ENTRIES, 8, LANES)),
             dma((runs + 4,)),
             dma,

time: 49.4 us -> 48.9 us (0.990)
  Pallas kernels: 46.1 us -> 45.6 us
    pallas_call x1, Pallas kernels: 46.1 us -> 45.6 us  [local(): pl.pallas_call(kernel, name='energy_score', out_shape=(pltpu.VMEM((rows,...]
where the time goes in v9:
time: 48.9 us; the launch traced here: 48.8 us
  Pallas kernels  45.6 us (93%)
  between operations  2.33 us (5%)
  local copies, waits for them, and re-layouts  0.89 us (2%)
    pallas_call x1, Pallas kernels, local(): pl.pallas_call(kernel, name='energy_score', out_shape=(pltpu.VMEM((rows,...  45.6 us

profile of v9, /device:TPU:1, one launch (start us, length us, event | category | flops | bytes accessed | tf_op | source)
XLA Modules:
  0.0 48.8 jit_solution(1289713831857586384)
XLA Ops:
  0.6 45.6 %energy_score.1 = (f32[100,16,128]{2,1,0:T(8,128)S(1)}, f32[1,1]{1,0:T(1,128)}) custom-call(s32[33]{0:T(128)} %starts_in.1, f32[100]{0:T(128)} %penalty_in.1, f32[4,25,32,128]{3,2,1,0:T(8,128)} %bitcast.5, f32[100,4096]{1,0:T(8,128)} %truth.1, f32[32,128]{1,0:T(8,128)} %bitcast.6), custom_call_target="tpu_custom_call" | custom-call | tf_op jit(solution)/shard_map/energy_score/pallas_call | solution.py:418
  46.2 0.9 %copy.11 = f32[1,100,2048]{2,0,1:T(1,128)} copy(f32[1,100,2048]{2,0,1:T(1,128)S(1)} %bitcast.4) | data formatting | bytes 1638400
